TPU v7x, 256 devices: a whole 4x4x8 slice. The times are simulated.
256 devices in a mesh: section: 2 (over core), grp: 4 (over y), ctx: 32 (over x, z).
Axes of the slice: x: 4, y: 4, z: 8, core: 2. Of those that a mesh axis runs over, the one named last changes fastest.
Arguments:
- q_pf: bfloat16 [2, 4, 4096, 4096], P('section', 'grp', 'ctx'), may hold values from -16 to 16
- k_pf: bfloat16 [2, 4, 4096, 1024], P('section', 'grp', 'ctx'), may hold values from -16 to 16
- v_pf: bfloat16 [2, 4, 4096, 1024], P('section', 'grp', 'ctx'), may hold values from -6 to 6
- pf_blocks: int32 [2, 4, 2], P(None, 'grp'), may hold values from 1 to 192, 256 in all within a row
- slot_order: int32 [2, 4, 16], P(None, 'grp'), may hold values from 0 to 15, each once within a row
- cache_k: bfloat16 [2, 4, 128, 4096, 128], P('section', 'grp', 'ctx'), may hold values from -6 to 6
- cache_v: bfloat16 [2, 4, 128, 4096, 128], P('section', 'grp', 'ctx'), may hold values from -6 to 6
- ctx_len: int32 [2, 4, 16], P('section', 'grp'), may hold values from 1 to 4096
- q_dec: bfloat16 [2, 4, 128, 4, 512], P('section', 'grp', 'ctx'), may hold values from -16 to 16
- k_new: bfloat16 [2, 4, 128, 4, 128], P('section', 'grp', 'ctx'), may hold values from -16 to 16
- v_new: bfloat16 [2, 4, 128, 4, 128], P('section', 'grp', 'ctx'), may hold values from -6 to 6
Outputs:
- pf_out: bfloat16 [2, 4, 4096, 4096], P('section', 'grp', 'ctx')
- dec_out: bfloat16 [2, 4, 128, 4, 512], P('section', 'grp', 'ctx')
Inputs may be any that keep to these rules, and one draw needn't show every extreme that they name: `pf_blocks`: the 2 counts of a row sum to 256.
All inputs are finite; a program needn't handle non-finite values.
Results may differ from a plain program's by a relative error of at most 0.0055.
Values may be sent and summed in bfloat16 or wider, within the bound.
No kernel may reach another device: no remote copies, remote signals or barrier semaphores. Data moves between devices by JAX's collectives and lax.ppermute only.
A program may use at most 128 MiB of HBM per device.

v0:
```python
import math

import jax
import jax.numpy as jnp
from jax import lax
from jax.sharding import PartitionSpec as P

BLOCK = 16


masked_score = -1e30


def from_partner(value, axis, stride):
    mask = 2**stride
    pairs = [(source, source ^ mask) for source in range(lax.axis_size(axis))]
    return lax.ppermute(value, axis, pairs)


def span_layout(block_counts, token_total):
    req_lengths = block_counts * BLOCK
    req_ends = jnp.cumsum(req_lengths)
    req_starts = req_ends - req_lengths
    positions = jnp.arange(token_total, dtype=jnp.int32)
    owners = jnp.sum((positions[:, None] >= req_ends[None, :]).astype(jnp.int32), axis=1)
    return (req_lengths, req_starts, owners)


def decode_rows(query_rows, keys_full, values_full, fresh_keys, fresh_values, live_len, group_size):
    row_count, step_count, query_width = query_rows.shape
    head_dim = fresh_keys.shape[-1]
    context = keys_full.shape[1]
    queries = query_rows.reshape(row_count, step_count, group_size, head_dim)
    inv_root = 1.0 / math.sqrt(head_dim)
    cache_ok = (jnp.arange(context, dtype=jnp.int32)[None, :] < live_len[:, None])[:, None, None, :]
    step_ids = jnp.arange(step_count, dtype=jnp.int32)
    fresh_ok = (step_ids[None, :] <= step_ids[:, None])[None, :, None, :]
    cache_scores = (
        jnp.einsum("ntrd,ncd->ntrc", queries, keys_full, preferred_element_type=jnp.float32)
        * inv_root
    )
    cache_scores = jnp.where(cache_ok, cache_scores, masked_score)
    fresh_scores = (
        jnp.einsum("ntrd,nud->ntru", queries, fresh_keys, preferred_element_type=jnp.float32)
        * inv_root
    )
    fresh_scores = jnp.where(fresh_ok, fresh_scores, masked_score)
    row_max = jnp.maximum(jnp.max(cache_scores, axis=-1), jnp.max(fresh_scores, axis=-1))[..., None]
    cache_w = jnp.where(cache_ok, jnp.exp(cache_scores - row_max), 0.0)
    fresh_w = jnp.where(fresh_ok, jnp.exp(fresh_scores - row_max), 0.0)
    row_sum = jnp.sum(cache_w, axis=-1) + jnp.sum(fresh_w, axis=-1)
    weighted = jnp.einsum(
        "ntrc,ncd->ntrd",
        cache_w.astype(jnp.bfloat16),
        values_full,
        preferred_element_type=jnp.float32,
    )
    weighted = weighted + jnp.einsum(
        "ntru,nud->ntrd",
        fresh_w.astype(jnp.bfloat16),
        fresh_values,
        preferred_element_type=jnp.float32,
    )
    return (
        (weighted / row_sum[..., None])
        .astype(jnp.bfloat16)
        .reshape(row_count, step_count, query_width)
    )


def per_device(
    q_pf, k_pf, v_pf, pf_blocks, slot_order, cache_k, cache_v, ctx_len, q_dec, k_new, v_new
):
    head_dim = k_new.shape[-1]
    kv_heads = k_pf.shape[-1] // head_dim
    q_heads = q_pf.shape[-1] // head_dim
    group_size = q_heads // kv_heads
    tok_dev = q_pf.shape[2]
    shards = lax.axis_size("ctx")
    token_total = tok_dev * shards
    pf_count = pf_blocks.shape[-1]
    rows_dev = cache_k.shape[2]
    context = cache_k.shape[3]
    slots_total = slot_order.shape[-1]
    slots_dev = min(rows_dev, slots_total)
    heads_here = rows_dev // slots_dev
    own_pool = lax.axis_index("section")
    other_pool = 1 - own_pool
    shard_index = lax.axis_index("ctx")
    req_lengths, req_starts, owners = span_layout(pf_blocks[own_pool, 0], token_total)
    queries = q_pf[0, 0].reshape(tok_dev, q_heads, head_dim)
    key_rows = k_pf[0, 0].reshape(tok_dev, kv_heads, head_dim)
    value_rows = v_pf[0, 0].reshape(tok_dev, kv_heads, head_dim)
    inv_root = 1.0 / math.sqrt(head_dim)
    local_first = shard_index * tok_dev
    my_owner = lax.dynamic_slice_in_dim(owners, local_first, tok_dev, 0)
    my_pos = local_first + jnp.arange(tok_dev, dtype=jnp.int32)
    grouped_q = queries.reshape(tok_dev, kv_heads, group_size, head_dim)
    initial = (
        jnp.full((kv_heads, group_size, tok_dev), masked_score, jnp.float32),
        jnp.zeros((kv_heads, group_size, tok_dev), jnp.float32),
        jnp.zeros((kv_heads, group_size, tok_dev, head_dim), jnp.float32),
    )
    folded = initial
    piece_keys = lax.all_gather(key_rows, "ctx", axis=0, tiled=True)
    piece_values = lax.all_gather(value_rows, "ctx", axis=0, tiled=True)
    key_count = piece_keys.shape[0]
    step_rows = math.gcd(key_count, 512)

    def one_step(running, block_index):
        first_row = block_index * step_rows
        block_keys = lax.dynamic_slice_in_dim(piece_keys, first_row, step_rows, 0)
        block_values = lax.dynamic_slice_in_dim(piece_values, first_row, step_rows, 0)
        key_pos = first_row + jnp.arange(step_rows, dtype=jnp.int32)
        key_owner = lax.dynamic_slice_in_dim(owners, first_row, step_rows, 0)
        allowed = (key_owner[None, :] == my_owner[:, None]) & (key_pos[None, :] <= my_pos[:, None])

        def attend(current):
            run_max, run_sum, run_acc = current
            scores = (
                jnp.einsum(
                    "qhrd,khd->hrqk", grouped_q, block_keys, preferred_element_type=jnp.float32
                )
                * inv_root
            )
            scores = jnp.where(allowed[None, None], scores, masked_score)
            next_max = jnp.maximum(run_max, jnp.max(scores, axis=-1))
            weights = jnp.where(allowed[None, None], jnp.exp(scores - next_max[..., None]), 0.0)
            rescale = jnp.exp(run_max - next_max)
            next_sum = run_sum * rescale + jnp.sum(weights, axis=-1)
            next_acc = run_acc * rescale[..., None] + jnp.einsum(
                "hrqk,khd->hrqd",
                weights.astype(jnp.bfloat16),
                block_values,
                preferred_element_type=jnp.float32,
            )
            return (next_max, next_sum, next_acc)

        def unchanged(current):
            return current

        return (lax.cond(jnp.any(allowed), attend, unchanged, running), None)

    folded, ignored = lax.scan(
        one_step, folded, jnp.arange(key_count // step_rows, dtype=jnp.int32)
    )
    run_max, run_sum, run_acc = folded
    attended = (run_acc / run_sum[..., None]).astype(jnp.bfloat16)
    pf_result = attended.transpose(2, 0, 1, 3).reshape(tok_dev, q_heads * head_dim)
    block_count = tok_dev // BLOCK
    own_slots = slot_order[own_pool, 0]
    block_owner = my_owner.reshape(block_count, BLOCK)[:, 0]
    req_ids = jnp.arange(pf_count, dtype=jnp.int32)
    block_slot = jnp.sum(
        (block_owner[:, None] == req_ids[None, :]).astype(jnp.int32) * own_slots[None, :pf_count],
        axis=1,
    )
    dest_ids = jnp.arange(shards, dtype=jnp.int32)
    dest_low = dest_ids * rows_dev % slots_total
    accept = (block_slot[None, :] >= dest_low[:, None]) & (
        block_slot[None, :] < dest_low[:, None] + slots_dev
    )

    def outgoing(rows_in):
        blocks = rows_in.reshape(block_count, BLOCK, kv_heads, head_dim)
        spread = jnp.repeat(blocks.transpose(2, 0, 1, 3), shards // kv_heads, axis=0)[
            :, :, :, None, :
        ]
        return jnp.where(accept[:, :, None, None, None], spread, jnp.zeros_like(spread))

    sent_k, sent_v = (
        lax.all_to_all(outgoing(key_rows), "ctx", split_axis=0, concat_axis=0, tiled=True),
        lax.all_to_all(outgoing(value_rows), "ctx", split_axis=0, concat_axis=0, tiled=True),
    )
    span_k = sent_k.reshape(token_total, heads_here, head_dim)
    span_v = sent_v.reshape(token_total, heads_here, head_dim)
    landed = from_partner(jnp.stack([span_k, span_v]), "section", 0)
    other_lengths, other_starts, ignored_owner = span_layout(pf_blocks[other_pool, 0], token_total)
    taken_slots = slot_order[other_pool, 0, :pf_count]
    slot_first = shard_index * rows_dev % slots_total
    my_slots = slot_first + jnp.arange(slots_dev, dtype=jnp.int32)
    matches = (taken_slots[None, :] == my_slots[:, None]).astype(jnp.int32)
    is_new = jnp.sum(matches, axis=1) > 0
    new_start = jnp.sum(matches * other_starts[None, :], axis=1)
    new_length = jnp.sum(matches * other_lengths[None, :], axis=1)
    old_lengths = lax.dynamic_slice_in_dim(ctx_len[0, 0], slot_first, slots_dev, 0)
    live_len = jnp.where(is_new, new_length, old_lengths)
    cache_pos = jnp.arange(context, dtype=jnp.int32)
    source = jnp.clip(new_start[:, None] + cache_pos[None, :], 0, token_total - 1)
    use_new = is_new[:, None] & (cache_pos[None, :] < new_length[:, None])
    gathered = landed[:, source].transpose(0, 3, 1, 2, 4).reshape(2, rows_dev, context, head_dim)
    use_rows = jnp.tile(use_new, (heads_here, 1))[:, :, None]
    keys_full = jnp.where(use_rows, gathered[0], cache_k[0, 0])
    values_full = jnp.where(use_rows, gathered[1], cache_v[0, 0])
    dec_result = decode_rows(
        q_dec[0, 0],
        keys_full,
        values_full,
        k_new[0, 0],
        v_new[0, 0],
        jnp.tile(live_len, heads_here),
        group_size,
    )
    return (pf_result[None, None], dec_result[None, None])


def solution(mesh):
    return jax.shard_map(
        per_device,
        mesh=mesh,
        in_specs=(
            P("section", "grp", "ctx", None),
            P("section", "grp", "ctx", None),
            P("section", "grp", "ctx", None),
            P(None, "grp", None),
            P(None, "grp", None),
            P("section", "grp", "ctx", None, None),
            P("section", "grp", "ctx", None, None),
            P("section", "grp", None),
            P("section", "grp", "ctx", None, None),
            P("section", "grp", "ctx", None, None),
            P("section", "grp", "ctx", None, None),
        ),
        out_specs=(P("section", "grp", "ctx", None), P("section", "grp", "ctx", None, None)),
        check_vma=False,
    )
```

profile of v0, /device:TPU:223, one launch (start us, length us, event | category | flops | bytes accessed | tf_op | source)
XLA Modules:
  0.0 343.2 jit_solution(8075374810972975172)
XLA Ops:
  16.6 36.8 %all_to_all.10 = bf16[32,8,16,1,128]{4,2,1,3,0:T(8,128)(2,1)} all-to-all(bf16[32,8,16,1,128]{4,2,1,3,0:T(8,128)(2,1)S(1)} %bitcast.173), channel_id=1, replica_groups=mesh['section'=2,'grp'=4,'ctx'=32] {'ctx'}, dimensions={0} | all-to-all | bytes 2097152 | tf_op jit(solution)/shard_map/all_to_all | solution.py:173
  53.4 10.2 %all-to-all-start = ((bf16[32,8,16,1,128]{4,2,1,3,0:T(8,128)(2,1)}), bf16[32,8,16,1,128]{4,2,1,3,0:T(8,128)(2,1)}, u32[]{:S(2)}, u32[]{:S(2)}) async-start(bf16[32,8,16,1,128]{4,2,1,3,0:T(8,128)(2,1)} %bitcast.17), calls=%async_computation | async-start | bytes 2097152 | tf_op jit(solution)/shard_map/all_to_all | solution.py:172
  65.5 3.2 copy.78
  68.6 21.1 %all-to-all-done = bf16[32,8,16,1,128]{4,2,1,3,0:T(8,128)(2,1)} async-done(((bf16[32,8,16,1,128]{4,2,1,3,0:T(8,128)(2,1)}), bf16[32,8,16,1,128]{4,2,1,3,0:T(8,128)(2,1)}, u32[]{:S(2)}, u32[]{:S(2)}) %all-to-all-start) | async-done | bytes 1048608 | tf_op jit(solution)/shard_map/all_to_all | solution.py:172
  89.8 3.2 copy.77
  92.9 4.8 %pad_maximum_fusion = bf16[2,4096,1,128]{3,0,1,2:T(2,128)(2,1)S(1)} fusion(bf16[1,4096,1,128]{3,0,1,2:T(2,128)(2,1)S(1)} %copy.78, bf16[1,4096,1,128]{3,0,1,2:T(2,128)(2,1)S(1)} %copy.77), kind=kLoop, calls=%fused_computation.40 | loop fusion | flops 4194304 | bytes 4194304 | tf_op jit(solution)/shard_map/stack | solution.py:177
  97.8 5.1 %collective-permute-start = (bf16[2,4096,1,128]{3,0,1,2:T(2,128)(2,1)S(1)}, bf16[2,4096,1,128]{3,0,1,2:T(2,128)(2,1)S(1)}, u32[]{:S(2)}, u32[]{:S(2)}) collective-permute-start(bf16[2,4096,1,128]{3,0,1,2:T(2,128)(2,1)S(1)} %pad_maximum_fusion), channel_id=1, source_target_pairs={{0,128},{128,0},{1,129},{129,1},{2,130},{130,2},{3,131},{131,3},{4... | collective-permute-start | bytes 6291464 | tf_op jit(solution)/shard_map/ppermute | solution.py:17
  103.3 3.3 collective-permute-done
  106.6 106.3 %gather_fusion = bf16[16384,2,128]{2,1,0:T(2,128)(2,1)} fusion(bf16[2,4096,128]{2,0,1:T(2,128)(2,1)S(1)} %bitcast.168, s32[16384]{0:T(1024)S(1)} %broadcast_clamp_fusion), kind=kCustom, calls=%fused_computation | custom fusion | bytes 16842752 | tf_op jit(solution)/shard_map/gather | solution.py:191
  212.9 7.9 %copy.95 = bf16[4,4096,2,128]{3,1,0,2:T(8,128)(2,1)} copy(bf16[4,4096,2,128]{3,2,1,0:T(2,128)(2,1)} %bitcast.167) | data formatting | bytes 16777216 | tf_op jit(solution)/shard_map/gather | solution.py:191
  220.9 6.1 %fusion.76 = (f32[4,4,4]{2,1,0:T(4,128)S(1)}, f32[4,4,4,4096]{3,2,1,0:T(4,128)S(1)}) fusion(bf16[4,4,4,128]{3,2,1,0:T(4,128)(2,1)S(1)} %reshape_squeeze.11, bf16[2,4,4096,128]{3,2,1,0:T(8,128)(2,1)} %bitcast.169, bf16[1,1,4,4096,128]{4,3,2,1,0:T(8,128)(2,1)S(1)} %copy-done.7, pred[4,4096]{1,0:T(4,128)(4,1)S(1)} %fusion.51, ...), kind=kOutput, calls=%fused_computation.109 | convolution fusion | flops 69992384 | bytes 9486592 | tf_op jit(solution)/shard_map/ntrd,ncd->ntrc/dot_general | solution.py:39
  228.1 3.3 fusion.40
  232.0 11.9 %copy.68 = bf16[4096,8,128]{2,0,1:T(8,128)(2,1)} copy(bf16[4096,8,128]{0,2,1:T(8,128)(2,1)} %all-gather.3.cloned.1.call-done) | data formatting | bytes 16777216
  244.0 11.9 %copy.70 = bf16[4096,8,128]{2,0,1:T(8,128)(2,1)} copy(bf16[4096,8,128]{0,2,1:T(8,128)(2,1)} %all-gather.5.cloned.1.call-done) | data formatting | bytes 16777216
  256.1 77.1 %while.15 = (s32[]{:T(128)}, f32[8,4,128]{2,1,0:T(4,128)S(1)}, f32[8,4,128]{2,1,0:T(4,128)S(1)}, f32[8,4,128,128]{3,2,1,0:T(8,128)S(1)}, s32[8]{0:T(128)S(1)}, /...) while((s32[]{:T(128)}, f32[8,4,128]{2,1,0:T(4,128)S(1)}, ...), condition=%wide.region_8.9_spmd.clone, body=%wide.region_2.8_spmd.clone.sunk | while | flops 1102324352 | bytes 33043288 | solution.py:144
  264.4 9.2 %conditional.3 = ((f32[8,4,128]{2,1,0:T(4,128)S(1)}, f32[8,4,128]{2,1,0:T(4,128)S(1)}, f32[8,4,128,128]{3,2,1,0:T(8,128)S(1)})) conditional(s32[]{:T(128)} %convert_element_type.53, (f32[8,4,128]{2,1,0:T(4,128)S(1)}, f32[8,4,128]{2,1,0:T(4,128)S(1)}, f32[8,4,128,128]{3,2,1,0:T(8,128)S(1)}) %tuple.60, (pred[128,512]{0,1:T(8,128)(4,1)S(1)}, ...), branch_computations={%region_4.4_spmd, %region_5.7_spmd} | conditional | flops 1102061568 | bytes 32965664 | solution.py:142
  264.4 2.6 fusion.2
  269.2 4.4 %multiply_add_fusion = f32[8,4,128,128]{3,2,1,0:T(8,128)S(1)} fusion(f32[8,4,128,128]{3,2,1,0:T(8,128)S(1)} %get-tuple-element.113, f32[8,512,128,4]{2,1,3,0:T(8,128)S(1)} %get-tuple-element.238, f32[8,4,128]{2,1,0:T(4,128)S(1)} %max.15, pred[128,512]{0,1:T(8,128)(4,1)S(1)} %get-tuple-element.108, bf16[4096,8,128]{2,0,1:T(8,128)(2,1)} %get-tuple-element.114, ...), kind=kOutput, calls=%fused_computation.9 | convolution fusion | flops 548405248 | bytes 13730304 | tf_op jit(solution)/shard_map/while/body/eval_jaxpr/cond/branch_1_fun/hrqk,khd->hrqd/dot_general | solution.py:131
  276.3 9.2 %conditional.3 = ((f32[8,4,128]{2,1,0:T(4,128)S(1)}, f32[8,4,128]{2,1,0:T(4,128)S(1)}, f32[8,4,128,128]{3,2,1,0:T(8,128)S(1)})) conditional(s32[]{:T(128)} %convert_element_type.53, (f32[8,4,128]{2,1,0:T(4,128)S(1)}, f32[8,4,128]{2,1,0:T(4,128)S(1)}, f32[8,4,128,128]{3,2,1,0:T(8,128)S(1)}) %tuple.60, (pred[128,512]{0,1:T(8,128)(4,1)S(1)}, ...), branch_computations={%region_4.4_spmd, %region_5.7_spmd} | conditional | flops 1102061568 | bytes 32965664 | solution.py:142
  276.4 2.6 fusion.2
  281.1 4.4 %multiply_add_fusion = f32[8,4,128,128]{3,2,1,0:T(8,128)S(1)} fusion(f32[8,4,128,128]{3,2,1,0:T(8,128)S(1)} %get-tuple-element.113, f32[8,512,128,4]{2,1,3,0:T(8,128)S(1)} %get-tuple-element.238, f32[8,4,128]{2,1,0:T(4,128)S(1)} %max.15, pred[128,512]{0,1:T(8,128)(4,1)S(1)} %get-tuple-element.108, bf16[4096,8,128]{2,0,1:T(8,128)(2,1)} %get-tuple-element.114, ...), kind=kOutput, calls=%fused_computation.9 | convolution fusion | flops 548405248 | bytes 13730304 | tf_op jit(solution)/shard_map/while/body/eval_jaxpr/cond/branch_1_fun/hrqk,khd->hrqd/dot_general | solution.py:131
  288.3 9.2 %conditional.3 = ((f32[8,4,128]{2,1,0:T(4,128)S(1)}, f32[8,4,128]{2,1,0:T(4,128)S(1)}, f32[8,4,128,128]{3,2,1,0:T(8,128)S(1)})) conditional(s32[]{:T(128)} %convert_element_type.53, (f32[8,4,128]{2,1,0:T(4,128)S(1)}, f32[8,4,128]{2,1,0:T(4,128)S(1)}, f32[8,4,128,128]{3,2,1,0:T(8,128)S(1)}) %tuple.60, (pred[128,512]{0,1:T(8,128)(4,1)S(1)}, ...), branch_computations={%region_4.4_spmd, %region_5.7_spmd} | conditional | flops 1102061568 | bytes 32965664 | solution.py:142
  288.3 2.6 fusion.2
  293.0 4.4 %multiply_add_fusion = f32[8,4,128,128]{3,2,1,0:T(8,128)S(1)} fusion(f32[8,4,128,128]{3,2,1,0:T(8,128)S(1)} %get-tuple-element.113, f32[8,512,128,4]{2,1,3,0:T(8,128)S(1)} %get-tuple-element.238, f32[8,4,128]{2,1,0:T(4,128)S(1)} %max.15, pred[128,512]{0,1:T(8,128)(4,1)S(1)} %get-tuple-element.108, bf16[4096,8,128]{2,0,1:T(8,128)(2,1)} %get-tuple-element.114, ...), kind=kOutput, calls=%fused_computation.9 | convolution fusion | flops 548405248 | bytes 13730304 | tf_op jit(solution)/shard_map/while/body/eval_jaxpr/cond/branch_1_fun/hrqk,khd->hrqd/dot_general | solution.py:131
  300.2 9.2 %conditional.3 = ((f32[8,4,128]{2,1,0:T(4,128)S(1)}, f32[8,4,128]{2,1,0:T(4,128)S(1)}, f32[8,4,128,128]{3,2,1,0:T(8,128)S(1)})) conditional(s32[]{:T(128)} %convert_element_type.53, (f32[8,4,128]{2,1,0:T(4,128)S(1)}, f32[8,4,128]{2,1,0:T(4,128)S(1)}, f32[8,4,128,128]{3,2,1,0:T(8,128)S(1)}) %tuple.60, (pred[128,512]{0,1:T(8,128)(4,1)S(1)}, ...), branch_computations={%region_4.4_spmd, %region_5.7_spmd} | conditional | flops 1102061568 | bytes 32965664 | solution.py:142
  300.2 2.6 fusion.2
  305.0 4.4 %multiply_add_fusion = f32[8,4,128,128]{3,2,1,0:T(8,128)S(1)} fusion(f32[8,4,128,128]{3,2,1,0:T(8,128)S(1)} %get-tuple-element.113, f32[8,512,128,4]{2,1,3,0:T(8,128)S(1)} %get-tuple-element.238, f32[8,4,128]{2,1,0:T(4,128)S(1)} %max.15, pred[128,512]{0,1:T(8,128)(4,1)S(1)} %get-tuple-element.108, bf16[4096,8,128]{2,0,1:T(8,128)(2,1)} %get-tuple-element.114, ...), kind=kOutput, calls=%fused_computation.9 | convolution fusion | flops 548405248 | bytes 13730304 | tf_op jit(solution)/shard_map/while/body/eval_jaxpr/cond/branch_1_fun/hrqk,khd->hrqd/dot_general | solution.py:131
  312.1 9.2 %conditional.3 = ((f32[8,4,128]{2,1,0:T(4,128)S(1)}, f32[8,4,128]{2,1,0:T(4,128)S(1)}, f32[8,4,128,128]{3,2,1,0:T(8,128)S(1)})) conditional(s32[]{:T(128)} %convert_element_type.53, (f32[8,4,128]{2,1,0:T(4,128)S(1)}, f32[8,4,128]{2,1,0:T(4,128)S(1)}, f32[8,4,128,128]{3,2,1,0:T(8,128)S(1)}) %tuple.60, (pred[128,512]{0,1:T(8,128)(4,1)S(1)}, ...), branch_computations={%region_4.4_spmd, %region_5.7_spmd} | conditional | flops 1102061568 | bytes 32965664 | solution.py:142
  312.1 2.6 fusion.2
  316.9 4.4 %multiply_add_fusion = f32[8,4,128,128]{3,2,1,0:T(8,128)S(1)} fusion(f32[8,4,128,128]{3,2,1,0:T(8,128)S(1)} %get-tuple-element.113, f32[8,512,128,4]{2,1,3,0:T(8,128)S(1)} %get-tuple-element.238, f32[8,4,128]{2,1,0:T(4,128)S(1)} %max.15, pred[128,512]{0,1:T(8,128)(4,1)S(1)} %get-tuple-element.108, bf16[4096,8,128]{2,0,1:T(8,128)(2,1)} %get-tuple-element.114, ...), kind=kOutput, calls=%fused_computation.9 | convolution fusion | flops 548405248 | bytes 13730304 | tf_op jit(solution)/shard_map/while/body/eval_jaxpr/cond/branch_1_fun/hrqk,khd->hrqd/dot_general | solution.py:131
  324.0 9.2 %conditional.3 = ((f32[8,4,128]{2,1,0:T(4,128)S(1)}, f32[8,4,128]{2,1,0:T(4,128)S(1)}, f32[8,4,128,128]{3,2,1,0:T(8,128)S(1)})) conditional(s32[]{:T(128)} %convert_element_type.53, (f32[8,4,128]{2,1,0:T(4,128)S(1)}, f32[8,4,128]{2,1,0:T(4,128)S(1)}, f32[8,4,128,128]{3,2,1,0:T(8,128)S(1)}) %tuple.60, (pred[128,512]{0,1:T(8,128)(4,1)S(1)}, ...), branch_computations={%region_4.4_spmd, %region_5.7_spmd} | conditional | flops 1102061568 | bytes 32965664 | solution.py:142
  328.8 4.4 %multiply_add_fusion = f32[8,4,128,128]{3,2,1,0:T(8,128)S(1)} fusion(f32[8,4,128,128]{3,2,1,0:T(8,128)S(1)} %get-tuple-element.113, f32[8,512,128,4]{2,1,3,0:T(8,128)S(1)} %get-tuple-element.238, f32[8,4,128]{2,1,0:T(4,128)S(1)} %max.15, pred[128,512]{0,1:T(8,128)(4,1)S(1)} %get-tuple-element.108, bf16[4096,8,128]{2,0,1:T(8,128)(2,1)} %get-tuple-element.114, ...), kind=kOutput, calls=%fused_computation.9 | convolution fusion | flops 548405248 | bytes 13730304 | tf_op jit(solution)/shard_map/while/body/eval_jaxpr/cond/branch_1_fun/hrqk,khd->hrqd/dot_general | solution.py:131
  (140 shorter events, 43.8 us)
Async XLA Ops:
  7.2 220.6 %copy-start = (bf16[1,1,4,4,128]{4,3,2,1,0:T(4,128)(2,1)S(1)}, bf16[1,1,4,4,128]{4,3,2,1,0:T(4,128)(2,1)}, u32[]{:S(2)}) copy-start(bf16[1,1,4,4,128]{4,3,2,1,0:T(4,128)(2,1)} %param.25) | copy-start | bytes 12292
  7.2 224.8 %all-gather.3.cloned.1.call-start = ((), (), s32[]{:S(2)}) async-start(), calls=%async_computation.2 | async-start | bytes 8650752 | tf_op jit(solution)/shard_map/all_gather | solution.py:105
  9.0 234.9 %all-gather.5.cloned.1.call-start = ((), (), s32[]{:S(2)}) async-start(), calls=%async_computation.3 | async-start | bytes 8650752 | tf_op jit(solution)/shard_map/all_gather | solution.py:106
  14.1 49.4 %copy-start.3 = (bf16[1,1,128,4096]{3,2,1,0:T(8,128)(2,1)S(1)}, bf16[1,1,128,4096]{3,2,1,0:T(8,128)(2,1)}, u32[]{:S(2)}) copy-start(bf16[1,1,128,4096]{3,2,1,0:T(8,128)(2,1)} %param.15) | copy-start | bytes 3145732
  16.5 48.4 %copy-start.4 = (bf16[1,1,4,4,512]{4,3,2,1,0:T(4,128)(2,1)S(1)}, bf16[1,1,4,4,512]{4,3,2,1,0:T(4,128)(2,1)}, u32[]{:S(2)}) copy-start(bf16[1,1,4,4,512]{4,3,2,1,0:T(4,128)(2,1)} %param.23) | copy-start | bytes 49156
  16.5 48.6 %copy-start.5 = (s32[2,1,2]{2,1,0:T(1,128)S(1)}, s32[2,1,2]{2,1,0:T(1,128)}, u32[]{:S(2)}) copy-start(s32[2,1,2]{2,1,0:T(1,128)} %param.18) | copy-start | bytes 52
  16.6 48.8 %copy-start.6 = (s32[1,1,16]{2,1,0:T(1,128)S(1)}, s32[1,1,16]{2,1,0:T(1,128)}, u32[]{:S(2)}) copy-start(s32[1,1,16]{2,1,0:T(1,128)} %param.22) | copy-start | bytes 196
  53.4 36.4 %all-to-all-start = ((bf16[32,8,16,1,128]{4,2,1,3,0:T(8,128)(2,1)}), bf16[32,8,16,1,128]{4,2,1,3,0:T(8,128)(2,1)}, u32[]{:S(2)}, u32[]{:S(2)}) async-start(bf16[32,8,16,1,128]{4,2,1,3,0:T(8,128)(2,1)} %bitcast.17), calls=%async_computation | async-start | bytes 2097152 | tf_op jit(solution)/shard_map/all_to_all | solution.py:172
  89.8 13.1 %copy-start.9 = (bf16[1,1,4,4,128]{4,3,2,1,0:T(4,128)(2,1)S(1)}, bf16[1,1,4,4,128]{4,3,2,1,0:T(4,128)(2,1)}, u32[]{:S(2)}) copy-start(bf16[1,1,4,4,128]{4,3,2,1,0:T(4,128)(2,1)} %param.24) | copy-start | bytes 12292
  97.8 8.9 %collective-permute-start = (bf16[2,4096,1,128]{3,0,1,2:T(2,128)(2,1)S(1)}, bf16[2,4096,1,128]{3,0,1,2:T(2,128)(2,1)S(1)}, u32[]{:S(2)}, u32[]{:S(2)}) collective-permute-start(bf16[2,4096,1,128]{3,0,1,2:T(2,128)(2,1)S(1)} %pad_maximum_fusion), channel_id=1, source_target_pairs={{0,128},{128,0},{1,129},{129,1},{2,130},{130,2},{3,131},{131,3},{4... | collective-permute-start | bytes 6291464 | tf_op jit(solution)/shard_map/ppermute | solution.py:17
  212.9 7.9 %copy-start.7 = (bf16[1,1,4,4096,128]{4,3,2,1,0:T(8,128)(2,1)S(1)}, bf16[1,1,4,4096,128]{4,3,2,1,0:T(8,128)(2,1)}, u32[]{:S(2)}) copy-start(bf16[1,1,4,4096,128]{4,3,2,1,0:T(8,128)(2,1)} %param.20) | copy-start | bytes 12582916
  220.9 7.2 %copy-start.2 = (bf16[4,4096,2,128]{3,1,0,2:T(8,128)(2,1)S(1)}, bf16[4,4096,2,128]{3,1,0,2:T(8,128)(2,1)}, u32[]{:S(2)}) copy-start(bf16[4,4096,2,128]{3,1,0,2:T(8,128)(2,1)} %copy.95) | copy-start | bytes 25165828
  220.9 7.2 %copy-start.8 = (bf16[1,1,4,4096,128]{4,3,2,1,0:T(8,128)(2,1)S(1)}, bf16[1,1,4,4096,128]{4,3,2,1,0:T(8,128)(2,1)}, u32[]{:S(2)}) copy-start(bf16[1,1,4,4096,128]{4,3,2,1,0:T(8,128)(2,1)} %param.21) | copy-start | bytes 12582916
  333.2 3.2 copy-start.1
Sparse Core Ops, SparseCore 0:
  10.5 123.9 all-gather.2
  137.0 100.8 all-gather.4
where the time goes:
time: 345 us; the launch traced here: 343 us
  local copies, waits for them, and re-layouts  161 us (47%)
  matrix products  52 us (15%)
  blocking collectives  36.8 us (11%)
  other arithmetic  28.5 us (8%)
  waiting for transfers between devices  24.5 us (7%)
  starting transfers between devices  15.3 us (4%)
  between operations  14.3 us (4%)
  loops' own time  10.5 us (3%)
    gather x2, local copies, waits for them, and re-layouts, per_device(): landed[:, source].transpose(0, 3, 1, 2, 4)  114 us
    all_to_all x1, blocking collectives, per_device(): lax.all_to_all(outgoing(value_rows), 'ctx', split_axis=0, concat_axis=0,...  36.8 us
    unnamed x29, local copies, waits for them, and re-layouts  30.9 us
    dot_general x6, matrix products, attend(): jnp.einsum('hrqk,khd->hrqd', weights.astype(jnp.bfloat16), block_values,...  26.4 us
    all_to_all x1, waiting for transfers between devices, per_device(): lax.all_to_all(outgoing(key_rows), 'ctx', split_axis=0, concat_axis=0, ti...  21.1 us
    dot_general x6, matrix products, attend(): jnp.einsum('qhrd,khd->hrqk', grouped_q, block_keys, preferred_element_typ...  15.7 us
    reduce_sum x6, other arithmetic, attend(): next_sum = run_sum * rescale + jnp.sum(weights, axis=-1)  12.4 us
    another operation x1, loops' own time, per_device(): lax.scan(one_step, folded, jnp.arange(key_count // step_rows, dtype=jnp.i...  10.2 us
  transfers between devices with their start and end apart: 4, of which 2 were waited for; matrix products, arithmetic and copies ran while one was open for 46% of the time, Pallas kernels for 0%

commit v1 on v0

v1 whole, which is shorter than its diff:
```python
import functools
import math

import jax
import jax.numpy as jnp
from jax import lax
from jax.experimental import pallas as pl
from jax.experimental.pallas import tpu as pltpu
from jax.sharding import PartitionSpec as P

HD = 128
BLOCK = 16
NX, NZ = 4, 8
ROWS = 128
XROWS = NZ * ROWS
HEADS = 2
RATIO = 4
STEPS = 4
SLOTS = 16
NEW = 4
MASKED = -1e30
SCALE = math.log2(math.e) / math.sqrt(HD)

ALONG_Z = [[x * NZ + z for z in range(NZ)] for x in range(NX)]
ALONG_X = [[x * NZ + z for x in range(NX)] for z in range(NZ)]

GRANT = 20 << 20

I_SECTION, I_CTX, I_BLOCKS, I_ORDER, I_LEN = 0, 1, 2, 6, 38


def nt(a, b):
    return lax.dot_general(a, b, (((1,), (1,)), ((), ())), preferred_element_type=jnp.float32)


def nn(a, b):
    return lax.dot_general(a, b, (((1,), (0,)), ((), ())), preferred_element_type=jnp.float32)


SAFE = 1e30


def stage_kernel(offsets, start, last, ints, q_ref, *refs):
    n = len(offsets)
    z = ints[I_CTX] % NZ
    first = ints[I_BLOCKS + 2 * ints[I_SECTION]] * BLOCK
    sources = [(z + d) % NZ for d in offsets]
    lanes = [slice(g * HD, (g + 1) * HD) for g in range(n)]
    heads = [slice(a * ROWS, (a + 1) * ROWS) for a in range(RATIO)]
    *refs, m_ref, l_ref = refs
    if start:
        *kvs, rows_out, acc_out = refs
    elif not last:
        *kvs, rows_in, acc_in, rows_out, acc_out = refs
    else:
        *kvs, low_half, high_half, rows_in, acc_in, out_ref, acc_end = refs

    def keys_values(h, c):
        def one(kv, at):
            return kv[pl.ds(at, 1), h].reshape(ROWS, 2 * HD)

        blocks = [one(kv, c) for kv in kvs]
        if last:
            half = NX // 2
            blocks.append(jnp.where(c < half, *[one(kv, c % half) for kv in (low_half, high_half)]))
        k = jnp.concatenate([b[:, :HD] for b in blocks], axis=0)
        v = jnp.concatenate([b[:, HD:] for b in blocks], axis=0)
        return k, v

    def block(x, carry):
        row0 = x * XROWS + z * ROWS
        low = jnp.where(row0 >= first, first // XROWS, 0)
        qx = q_ref[pl.ds(x, 1)].reshape(ROWS, HEADS * RATIO * HD)
        at = [slice(a * HD, (a + 1) * HD) for a in range(HEADS * RATIO)]
        qs = [
            jnp.concatenate([qx[:, at[h * RATIO + a]] for a in range(RATIO)], axis=0)
            for h in range(HEADS)
        ]
        spots = [h * NX + x for h in range(HEADS)]
        ms = [m_ref.at[h] for h in range(HEADS)]
        ls = [l_ref.at[h] for h in range(HEADS)]
        accs = [acc_end.at[h] if last else acc_out.at[spots[h]] for h in range(HEADS)]

        def allowed(c):
            row = row0 + lax.broadcasted_iota(jnp.int32, (ROWS, HD), 0)
            lane = c * XROWS + lax.broadcasted_iota(jnp.int32, (ROWS, HD), 1)
            begin = jnp.where(row < first, 0, first)
            return [(lane + src * ROWS <= row) & (lane + src * ROWS >= begin) for src in sources]

        def careful(c, held):
            ok = allowed(c)
            for h in range(HEADS):
                k, v = keys_values(h, c)
                s = nt(qs[h], k)
                ps = []
                for rs in heads:
                    cols = [jnp.where(o, s[rs, g], MASKED) for g, o in zip(lanes, ok)]
                    top = jnp.max(functools.reduce(jnp.maximum, cols), axis=-1, keepdims=True)
                    old = ms[h][rs] if held else None
                    new = jnp.maximum(old, top) if held else jnp.broadcast_to(top, (ROWS, HD))
                    pg = [jnp.exp2((t - new) * SCALE) for t in cols]
                    ms[h][rs] = new
                    total = functools.reduce(jnp.add, pg)
                    if held:
                        fix = jnp.exp2((old - new) * SCALE)
                        ls[h][rs] = ls[h][rs] * fix + total
                        accs[h][rs] = accs[h][rs] * fix
                    else:
                        ls[h][rs] = total
                    ps.append(jnp.concatenate([t.astype(jnp.bfloat16) for t in pg], axis=1))
                o = nn(jnp.concatenate(ps, axis=0), v)
                accs[h][...] = accs[h][...] + o if held else o

        def quick(c, masked):
            ok = allowed(c) if masked else None
            kvh = [keys_values(h, c) for h in range(HEADS)]
            scores = [nt(qs[h], kvh[h][0]) for h in range(HEADS)]
            for h in range(HEADS):
                s = scores[h]
                ps = []
                for rs in heads:
                    m = ms[h][rs]
                    pg = [jnp.exp2((s[rs, g] - m) * SCALE) for g in lanes]
                    if masked:
                        pg = [jnp.where(o, t, 0.0) for o, t in zip(ok, pg)]
                    ls[h][rs] += functools.reduce(jnp.add, pg)
                    ps.append(jnp.concatenate([t.astype(jnp.bfloat16) for t in pg], axis=1))
                accs[h][...] += nn(jnp.concatenate(ps, axis=0), kvh[h][1])

        def begin():
            if start:
                careful(x, False)
                return
            for h in range(HEADS):
                accs[h][...] = acc_in[pl.ds(spots[h], 1)].reshape(RATIO * ROWS, HD)
                given = rows_in[pl.ds(spots[h], 1)].reshape(8, RATIO * ROWS)
                ms[h][...] = jnp.broadcast_to(given[:1], (HD, RATIO * ROWS)).T
                ls[h][...] = jnp.broadcast_to(given[1:2] / HD, (HD, RATIO * ROWS)).T

        def quick_step(c, carry):
            near = (c < x) | functools.reduce(jnp.logical_and, [src < z for src in sources])
            whole = near & ((c * XROWS >= first) | (row0 + ROWS <= first))

            @pl.when(whole)
            def _():
                quick(c, False)

            @pl.when(jnp.logical_not(whole))
            def _():
                quick(c, True)

            return carry

        def careful_step(c, carry):
            careful(c, True)
            return carry

        end = x if start else x + 1
        begin()
        lax.fori_loop(low, end, quick_step, 0)

        @pl.when(jnp.logical_not(jnp.max(l_ref[...]) < SAFE))
        def _():
            begin()
            lax.fori_loop(low, end, careful_step, 0)

        for h in range(HEADS):
            if last:
                total = jnp.sum(ls[h][...], axis=-1, keepdims=True)
                o = (accs[h][...] / total).astype(jnp.bfloat16)
                for a, rs in enumerate(heads):
                    out_ref[pl.ds(x, 1), :, at[h * RATIO + a]] = o[rs][None]
            else:
                top = ms[h][...].T[:1]
                total = jnp.sum(ls[h][...].T, axis=0, keepdims=True)
                line = lax.broadcasted_iota(jnp.int32, (8, RATIO * ROWS), 0)
                rows_out[pl.ds(spots[h], 1)] = jnp.where(line == 0, top, total)[None]
        return carry

    lax.fori_loop(0, NX, block, 0)


def stage(ints, q, offsets, shards, ends=(), state=()):
    start, last = not state, bool(ends)
    rows = RATIO * ROWS

    def whole(array):
        return pl.BlockSpec(array.shape, lambda i, s: (0,) * len(array.shape))

    blocks = HEADS * NX
    held = [
        jax.ShapeDtypeStruct((blocks, 8, rows), jnp.float32),
        jax.ShapeDtypeStruct((blocks, rows, HD), jnp.float32),
    ]
    tile = pltpu.VMEM((HEADS, rows, HD), jnp.float32)
    grid = pltpu.PrefetchScalarGridSpec(
        num_scalar_prefetch=1,
        grid=(1,),
        in_specs=[whole(a) for a in (q, *shards, *ends, *state)],
        out_specs=whole(q) if last else [whole(a) for a in held],
        scratch_shapes=[tile] * (3 if last else 2),
    )
    pairs = 7 * HEADS * rows * ROWS * len(offsets)
    return pl.pallas_call(
        functools.partial(stage_kernel, offsets, start, last),
        grid_spec=grid,
        out_shape=jax.ShapeDtypeStruct(q.shape, q.dtype) if last else held,
        compiler_params=pltpu.CompilerParams(vmem_limit_bytes=GRANT),
        cost_estimate=pl.CostEstimate(
            flops=4 * HD * pairs, bytes_accessed=8 << 20, transcendentals=pairs
        ),
        name="prefill_begin" if start else "prefill_end" if last else "prefill_more",
    )(ints, q, *shards, *ends, *state)


def attend(q, parts):
    scores = [jnp.where(ok, nt(q, k), MASKED) for k, _, ok in parts]
    top = functools.reduce(jnp.maximum, [jnp.max(s, axis=-1, keepdims=True) for s in scores])
    total = acc = 0.0
    for s, (_, v, ok) in zip(scores, parts):
        p = jnp.where(ok, jnp.exp2((s - top) * SCALE), 0.0)
        total += jnp.sum(p, axis=-1, keepdims=True)
        acc += nn(p.astype(jnp.bfloat16), v)
    return (acc / total).astype(jnp.bfloat16)


def fresh_ok(rows):
    n = rows * STEPS * RATIO
    row = lax.broadcasted_iota(jnp.int32, (n, rows * STEPS), 0)
    key = lax.broadcasted_iota(jnp.int32, (n, rows * STEPS), 1)
    mine = row // (STEPS * RATIO) == key // STEPS
    return mine & (key % STEPS <= row // RATIO % STEPS)


def cached_kernel(ints, q_ref, kn_ref, vn_ref, k_ref, v_ref, out_ref):
    n = pl.program_id(0)
    slot = ints[I_CTX] * NEW % SLOTS + n
    length = ints[I_LEN + slot]
    q = q_ref[0]
    ok = lax.broadcasted_iota(jnp.int32, (q.shape[0], k_ref.shape[1]), 1) < length
    out_ref[0] = attend(q, [(k_ref[0], v_ref[0], ok), (kn_ref[0], vn_ref[0], fresh_ok(1))])


def decode_cached(ints, q, k_new, v_new, cache_k, cache_v):
    rows, context, _ = cache_k.shape
    n = q.shape[1]

    def whole(shape):
        return pl.BlockSpec((1,) + shape, lambda i, s: (i, 0, 0))

    grid = pltpu.PrefetchScalarGridSpec(
        num_scalar_prefetch=1,
        grid=(rows,),
        in_specs=[
            whole((n, HD)),
            whole((STEPS, HD)),
            whole((STEPS, HD)),
            whole((context, HD)),
            whole((context, HD)),
        ],
        out_specs=whole((n, HD)),
    )
    return pl.pallas_call(
        cached_kernel,
        grid_spec=grid,
        out_shape=jax.ShapeDtypeStruct(q.shape, jnp.bfloat16),
        compiler_params=pltpu.CompilerParams(vmem_limit_bytes=GRANT),
        cost_estimate=pl.CostEstimate(
            flops=4 * HD * rows * context * n,
            bytes_accessed=4 * rows * context * HD,
            transcendentals=rows * context * n,
        ),
        name="decode_cached",
    )(ints, q, k_new, v_new, cache_k, cache_v)


def taken_kernel(offsets, ints, q_ref, kn_ref, vn_ref, *refs):
    *kvs, end_low, end_high, out_ref = refs
    rows = q_ref.shape[0]
    n = rows * STEPS * RATIO
    section = ints[I_SECTION]
    first = ints[I_BLOCKS + 2 * section] * BLOCK
    slot0 = ints[I_CTX] * NEW % SLOTS
    z = ints[I_CTX] % NZ
    q = q_ref[...].reshape(n, HD)
    row = lax.broadcasted_iota(jnp.int32, (n, 1), 0) // (STEPS * RATIO)
    begin = jnp.zeros((n, 1), jnp.int32)
    stop = jnp.zeros((n, 1), jnp.int32)
    for i in range(2):
        mine = row == ints[I_ORDER + SLOTS * section + i] - slot0
        begin = jnp.where(mine, first * i, begin)
        stop = jnp.where(mine, first if i == 0 else NX * XROWS, stop)
    width = NX * ROWS
    col = lax.broadcasted_iota(jnp.int32, (n, width), 1)
    col = col // ROWS * XROWS + col % ROWS
    tail = jnp.concatenate([end_low[...], end_high[...]], axis=0)
    parts = []
    for d, kv in zip(offsets, [kv[...] for kv in kvs] + [tail]):
        token = col + (z + d) % NZ * ROWS
        kv = kv.reshape(width, 2 * HD)
        parts.append((kv[:, :HD], kv[:, HD:], (token >= begin) & (token < stop)))
    kn, vn = [r[...].reshape(rows * STEPS, HD) for r in (kn_ref, vn_ref)]
    out = attend(q, parts + [(kn, vn, fresh_ok(rows))])
    out_ref[...] = out.reshape(out_ref.shape)


def decode_taken(ints, q, k_new, v_new, shards, ends, offsets):
    def one_head(array):
        return pl.BlockSpec(
            (array.shape[0], pl.squeezed, ROWS, 2 * HD),
            lambda i, s: (0, s[I_CTX] % NZ // NEW, 0, 0),
        )

    def whole(array):
        return pl.BlockSpec(array.shape, lambda i, s: (0,) * array.ndim)

    grid = pltpu.PrefetchScalarGridSpec(
        num_scalar_prefetch=1,
        grid=(1,),
        in_specs=[whole(a) for a in (q, k_new, v_new)]
        + [one_head(a) for a in (*shards, *ends)],
        out_specs=whole(q),
    )
    keys = NX * XROWS
    n = q.shape[0] * q.shape[1]
    return pl.pallas_call(
        functools.partial(taken_kernel, offsets),
        grid_spec=grid,
        out_shape=jax.ShapeDtypeStruct(q.shape, jnp.bfloat16),
        compiler_params=pltpu.CompilerParams(vmem_limit_bytes=GRANT),
        cost_estimate=pl.CostEstimate(
            flops=4 * HD * keys * n, bytes_accessed=4 * keys * HD, transcendentals=keys * n
        ),
        name="decode_taken",
    )(ints, q, k_new, v_new, *shards, *ends)


def along_z(value, by):
    pairs = [(x * NZ + z, x * NZ + (z + by) % NZ) for x in range(NX) for z in range(NZ)]
    return lax.ppermute(value, "ctx", pairs)


def per_device(
    q_pf, k_pf, v_pf, pf_blocks, slot_order, cache_k, cache_v, ctx_len, q_dec, k_new, v_new
):
    section = lax.axis_index("section")
    ctx = lax.axis_index("ctx")
    ints = jnp.concatenate(
        [
            jnp.stack([section, ctx]).astype(jnp.int32),
            pf_blocks.reshape(-1),
            slot_order.reshape(-1),
            ctx_len.reshape(-1),
        ]
    )
    swap = [(0, 1), (1, 0)]
    together = lax.optimization_barrier

    def along_x(value):
        return lax.all_to_all(value, "ctx", 0, 0, axis_index_groups=ALONG_X, tiled=True)

    k, v, q = k_pf[0, 0], v_pf[0, 0], q_pf[0, 0]

    def cols(array, head):
        return array[:, head * HD : (head + 1) * HD]

    packed = jnp.stack(
        [
            jnp.concatenate([cols(a, HEADS * x + h) for a in (k, v)], axis=1)
            for x in range(NX)
            for h in range(HEADS)
        ]
    ).reshape(NX, HEADS, ROWS, 2 * HD)
    own_kv = along_x(packed)
    q, own_kv = together((q, own_kv))
    width = HEADS * RATIO * HD
    queries = jnp.stack([q[:, x * width : (x + 1) * width] for x in range(NX)])

    up1, down1 = along_z(own_kv, 1), along_z(own_kv, -1)
    up1, down1, queries, ints = together((up1, down1, queries, ints))
    up2, down2 = along_z(up1, 1), along_z(down1, -1)
    queries = along_x(queries)
    qd, kn, vn = q_dec[0, 0], k_new[0, 0], v_new[0, 0]
    rows = qd.shape[0]
    lists = (rows, STEPS * RATIO, HD)
    own = decode_cached(ints, qd.reshape(lists), kn, vn, cache_k[0, 0], cache_v[0, 0])
    fresh = lax.ppermute(jnp.concatenate([qd, kn, vn], axis=-1), "section", swap)
    up2, down2, own, fresh = together((up2, down2, own, fresh))
    up3, down3 = along_z(up2, 1), along_z(down2, -1)
    near, near_at = [own_kv, up1, down1, up2, down2], [0, -1, 1, -2, 2]
    lines, acc = stage(ints, queries, near_at, near)
    up3, down3, lines = together((up3, down3, lines))
    ends = [along_z(up3[: NX // 2], 1), along_z(down3[NX // 2 :], -1)]
    far, far_at, end_at = [up3, down3], [-3, 3], [4]
    out = stage(ints, queries, far_at + end_at, far, ends, (lines, acc))

    their_q = fresh[..., : RATIO * HD].reshape(lists)
    their_k = fresh[..., RATIO * HD : (RATIO + 1) * HD]
    their_v = fresh[..., (RATIO + 1) * HD :]
    their_q, out = together((their_q, out))
    theirs = decode_taken(
        ints, their_q, their_k, their_v, near + far, ends, near_at + far_at + end_at
    )
    out = along_x(out)
    pf_result = jnp.concatenate([out[x] for x in range(NX)], axis=1)
    back = lax.ppermute(theirs, "section", swap)
    slots = (ctx * rows) % SLOTS + jnp.arange(rows, dtype=jnp.int32)
    taken = slot_order[1 - section, 0, :2]
    is_new = jnp.any(slots[:, None] == taken[None, :], axis=1)
    dec_result = jnp.where(is_new[:, None, None], back, own).reshape(qd.shape)
    return (pf_result[None, None], dec_result[None, None])


def solution(mesh):
    return jax.shard_map(
        per_device,
        mesh=mesh,
        in_specs=(
            P("section", "grp", "ctx", None),
            P("section", "grp", "ctx", None),
            P("section", "grp", "ctx", None),
            P(None, "grp", None),
            P(None, "grp", None),
            P("section", "grp", "ctx", None, None),
            P("section", "grp", "ctx", None, None),
            P("section", "grp", None),
            P("section", "grp", "ctx", None, None),
            P("section", "grp", "ctx", None, None),
            P("section", "grp", "ctx", None, None),
        ),
        out_specs=(P("section", "grp", "ctx", None), P("section", "grp", "ctx", None, None)),
        check_vma=False,
    )
```

time: 345 us -> 122 us (0.35)
  the two profiles are of different devices: /device:TPU:223 before, /device:TPU:8 now
where the time goes in v1:
time: 122 us
  Pallas kernels  34.6 us (28%)
  waiting for transfers between devices  28.7 us (24%)
  starting transfers between devices  23.5 us (19%)
  local copies, waits for them, and re-layouts  16.6 us (14%)
  blocking collectives  13.6 us (11%)
  other arithmetic  3.84 us (3%)
    pallas_call x2, Pallas kernels, stage(): pl.pallas_call(functools.partial(stage_kernel, offsets, start, last), gri...  28.3 us
    ppermute x8, waiting for transfers between devices, along_z(): return lax.ppermute(value, 'ctx', pairs)  17.7 us
    ppermute x8, starting transfers between devices, along_z(): return lax.ppermute(value, 'ctx', pairs)  14.4 us
    all_to_all x1, blocking collectives, along_x(): lax.all_to_all(value, 'ctx', 0, 0, axis_index_groups=ALONG_X, tiled=True)  13.6 us
    unnamed x39, local copies, waits for them, and re-layouts  11.8 us
    all_to_all x2, waiting for transfers between devices, along_x(): lax.all_to_all(value, 'ctx', 0, 0, axis_index_groups=ALONG_X, tiled=True)  10.4 us
    all_to_all x2, starting transfers between devices, along_x(): lax.all_to_all(value, 'ctx', 0, 0, axis_index_groups=ALONG_X, tiled=True)  8.11 us
    pallas_call x1, Pallas kernels, decode_cached(): pl.pallas_call(cached_kernel, grid_spec=grid, out_shape=jax.ShapeDtypeStr...  3.63 us
  transfers between devices with their start and end apart: 12, of which 7 were waited for; matrix products, arithmetic and copies ran while one was open for 3% of the time, Pallas kernels for 20%

profile of v1, /device:TPU:8, one launch (start us, length us, event | category | flops | bytes accessed | tf_op | source)
XLA Modules:
  0.0 121.8 jit_solution(16736892821482959300)
XLA Ops:
  0.7 1.1 fusion.8
  2.0 13.6 %all_to_all.15.refs_0_ = bf16[4,2,128,256]{3,2,1,0:T(8,128)(2,1)S(1)} all-to-all(bf16[4,2,128,256]{3,2,1,0:T(8,128)(2,1)S(1)} %bitcast.71), channel_id=1, replica_groups={{0,8,16,24},{1,9,17,25},{2,10,18,26},{3,11,19,27},{4,12,20,28},{5,13,21..., dimensions={0} | all-to-all | bytes 1048576 | tf_op jit(solution)/shard_map/all_to_all | solution.py:360
  15.5 5.9 %collective-permute-start.1 = (bf16[4,2,128,256]{3,2,1,0:T(8,128)(2,1)S(1)}, bf16[4,2,128,256]{3,2,1,0:T(8,128)(2,1)S(1)}, u32[]{:S(2)}, u32[]{:S(2)}) collective-permute-start(bf16[4,2,128,256]{3,2,1,0:T(8,128)(2,1)S(1)} %all_to_all.15.refs_0_), channel_id=1, source_target_pairs={{0,7},{1,0},{2,1},{3,2},{4,3},{5,4},{6,5},{7,6},{8,15},{9,8},{10,9... | collective-permute-start | bytes 1572872 | tf_op jit(solution)/shard_map/ppermute | solution.py:340
  22.7 0.7 reduce.7
  23.6 1.1 pad_maximum_fusion
  24.7 6.6 %collective-permute-done.1.refs_2_ = bf16[4,2,128,256]{3,2,1,0:T(8,128)(2,1)S(1)} collective-permute-done((bf16[4,2,128,256]{3,2,1,0:T(8,128)(2,1)S(1)}, bf16[4,2,128,256]{3,2,1,0:T(8,128)(2,1)S(1)}, u32[]{:S(2)}, u32[]{:S(2)}) %collective-permute-start.1) | collective-permute-done | bytes 524320 | tf_op jit(solution)/shard_map/ppermute | solution.py:340
  31.4 3.4 %collective-permute-done.refs_1_ = bf16[4,2,128,256]{3,2,1,0:T(8,128)(2,1)S(1)} collective-permute-done((bf16[4,2,128,256]{3,2,1,0:T(8,128)(2,1)S(1)}, bf16[4,2,128,256]{3,2,1,0:T(8,128)(2,1)S(1)}, u32[]{:S(2)}, u32[]{:S(2)}) %collective-permute-start) | collective-permute-done | bytes 524320 | tf_op jit(solution)/shard_map/ppermute | solution.py:340
  34.8 3.2 %collective-permute-start.3 = (bf16[4,2,128,256]{3,2,1,0:T(8,128)(2,1)S(1)}, bf16[4,2,128,256]{3,2,1,0:T(8,128)(2,1)S(1)}, u32[]{:S(2)}, u32[]{:S(2)}) collective-permute-start(bf16[4,2,128,256]{3,2,1,0:T(8,128)(2,1)S(1)} %collective-permute-done.1.refs_2_), channel_id=1, source_target_pairs={{0,7},{1,0},{2,1},{3,2},{4,3},{5,4},{6,5},{7,6},{8,15},{9,8},{10,9... | collective-permute-start | bytes 1572872 | tf_op jit(solution)/shard_map/ppermute | solution.py:340
  38.0 3.5 %all-to-all-start.1 = ((bf16[4,128,1024]{2,1,0:T(8,128)(2,1)}), bf16[4,128,1024]{2,1,0:T(8,128)(2,1)S(1)}, u32[]{:S(2)}, u32[]{:S(2)}) async-start(bf16[4,128,1024]{2,1,0:T(8,128)(2,1)} %pad_maximum_fusion), calls=%async_computation.1 | async-start | bytes 2097152 | tf_op jit(solution)/shard_map/all_to_all | solution.py:360
  41.7 2.2 %copy-done = bf16[1,1,4,4096,128]{4,3,2,1,0:T(8,128)(2,1)S(1)} copy-done((bf16[1,1,4,4096,128]{4,3,2,1,0:T(8,128)(2,1)S(1)}, bf16[1,1,4,4096,128]{4,3,2,1,0:T(8,128)(2,1)}, u32[]{:S(2)}) %copy-start) | copy-done | bytes 4194328
  43.9 2.2 %copy-done.1 = bf16[1,1,4,4096,128]{4,3,2,1,0:T(8,128)(2,1)S(1)} copy-done((bf16[1,1,4,4096,128]{4,3,2,1,0:T(8,128)(2,1)S(1)}, bf16[1,1,4,4096,128]{4,3,2,1,0:T(8,128)(2,1)}, u32[]{:S(2)}) %copy-start.1) | copy-done | bytes 4194328
  46.1 3.6 %decode_cached.1 = bf16[4,16,128]{2,1,0:T(8,128)(2,1)S(1)} custom-call(s32[54]{0:T(128)S(1)} %concatenate.41.ints, bf16[4,16,128]{2,1,0:T(8,128)(2,1)S(1)} %reshape_squeeze.3.q_ref, bf16[4,4,128]{2,1,0:T(4,128)(2,1)S(1)} %bitcast.69, bf16[4,4,128]{2,1,0:T(4,128)(2,1)S(1)} %bitcast.67, bf16[4,4096,128]{2,1,0:T(8,128)(2,1)S(1)} %bitcast.64, ...), custom_call_target="tpu_custom_call" | custom-call | flops 134217728 | bytes 8388608 | tf_op jit(solution)/shard_map/decode_cached/pallas_call | solution.py:263
  49.8 0.8 copy-done.9
  50.6 3.2 %collective-permute-start.6 = (bf16[4,2,128,256]{3,2,1,0:T(8,128)(2,1)}, bf16[4,2,128,256]{3,2,1,0:T(8,128)(2,1)S(1)}, u32[]{:S(2)}, u32[]{:S(2)}) collective-permute-start(bf16[4,2,128,256]{3,2,1,0:T(8,128)(2,1)} %copy-done.9), channel_id=1, source_target_pairs={{0,7},{1,0},{2,1},{3,2},{4,3},{5,4},{6,5},{7,6},{8,15},{9,8},{10,9... | collective-permute-start | bytes 1572872 | tf_op jit(solution)/shard_map/ppermute | solution.py:340
  54.0 1.0 copy-done.7
  55.0 1.0 copy-done.10
  56.0 17.8 %prefill_begin.1 = (f32[8,8,512]{2,1,0:T(8,128)S(1)}, f32[8,512,128]{2,1,0:T(8,128)S(1)}) custom-call(s32[54]{0:T(128)S(1)} %concatenate.41.ints, bf16[4,128,1024]{2,1,0:T(8,128)(2,1)S(1)} %all-to-all-done.1.q_ref, bf16[4,2,128,256]{3,2,1,0:T(8,128)(2,1)S(1)} %all_to_all.15.refs_0_, bf16[4,2,128,256]{3,2,1,0:T(8,128)(2,1)S(1)} %copy-done.7, ...), custom_call_target="tpu_custom_call" | custom-call | flops 2348810240 | bytes 8388608 | tf_op jit(solution)/shard_map/prefill_begin/pallas_call | solution.py:204
  73.8 1.3 %copy-done.2 = f32[8,512,128]{2,1,0:T(8,128)} copy-done((f32[8,512,128]{2,1,0:T(8,128)}, f32[8,512,128]{2,1,0:T(8,128)S(1)}, u32[]{:S(2)}) %copy-start.2) | copy-done | bytes 2097176
  75.2 0.7 slice.108
  75.9 0.7 slice.109
  76.6 2.0 %collective-permute-start.7 = (bf16[2,2,128,256]{3,2,1,0:T(8,128)(2,1)}, bf16[2,2,128,256]{3,2,1,0:T(8,128)(2,1)S(1)}, u32[]{:S(2)}, u32[]{:S(2)}) collective-permute-start(bf16[2,2,128,256]{3,2,1,0:T(8,128)(2,1)} %slice.108), channel_id=1, source_target_pairs={{0,1},{1,2},{2,3},{3,4},{4,5},{5,6},{6,7},{7,0},{8,9},{9,10},{10,1... | collective-permute-start | bytes 786440 | tf_op jit(solution)/shard_map/ppermute | solution.py:340
  78.7 6.4 %collective-permute-done.8.refs_3_.refs_8_ = bf16[2,2,128,256]{3,2,1,0:T(8,128)(2,1)S(1)} collective-permute-done((bf16[2,2,128,256]{3,2,1,0:T(8,128)(2,1)}, bf16[2,2,128,256]{3,2,1,0:T(8,128)(2,1)S(1)}, u32[]{:S(2)}, u32[]{:S(2)}) %collective-permute-start.8) | collective-permute-done | bytes 262176 | tf_op jit(solution)/shard_map/ppermute | solution.py:340
  85.1 1.2 collective-permute-done.7.refs_2_.refs_7_
  86.3 1.6 %copy-done.3 = f32[8,512,128]{2,1,0:T(8,128)S(1)} copy-done((f32[8,512,128]{2,1,0:T(8,128)S(1)}, f32[8,512,128]{2,1,0:T(8,128)}, u32[]{:S(2)}) %copy-start.3) | copy-done | bytes 2097176
  87.9 10.5 %prefill_end.1 = bf16[4,128,1024]{2,1,0:T(8,128)(2,1)} custom-call(s32[54]{0:T(128)S(1)} %concatenate.41.ints, bf16[4,128,1024]{2,1,0:T(8,128)(2,1)S(1)} %all-to-all-done.1.q_ref, bf16[4,2,128,256]{3,2,1,0:T(8,128)(2,1)S(1)} %collective-permute-done.5.refs_0_.refs_5_, bf16[4,2,128,256]{3,2,1,0:T(8,128)(2,1)S(1)} %collective-permute-done.6.refs_1_.refs_6_, ...), custom_call_target="tpu_custom_call" | custom-call | flops 1409286144 | bytes 8388608 | tf_op jit(solution)/shard_map/prefill_end/pallas_call | solution.py:204
  98.4 4.6 %all-to-all-start.2 = ((bf16[4,128,1024]{2,1,0:T(8,128)(2,1)}), bf16[4,128,1024]{2,1,0:T(8,128)(2,1)}, u32[]{:S(2)}, u32[]{:S(2)}) async-start(bf16[4,128,1024]{2,1,0:T(8,128)(2,1)} %prefill_end.1), calls=%async_computation.2 | async-start | bytes 2097152 | tf_op jit(solution)/shard_map/all_to_all | solution.py:360
  103.0 1.0 copy-done.11
  104.1 2.7 %decode_taken.1 = bf16[4,16,128]{2,1,0:T(8,128)(2,1)S(1)} custom-call(s32[54]{0:T(128)S(1)} %concatenate.41.ints, bf16[4,16,128]{2,1,0:T(8,128)(2,1)S(1)} %reshape.29.q_ref, bf16[4,4,128]{2,1,0:T(4,128)(2,1)S(1)} %get-tuple-element.61.kn_ref, bf16[4,4,128]{2,1,0:T(4,128)(2,1)S(1)} %get-tuple-element.60.vn_ref, ...), custom_call_target="tpu_custom_call" | custom-call | flops 134217728 | bytes 2097152 | tf_op jit(solution)/shard_map/decode_taken/pallas_call | solution.py:326
  106.7 1.0 collective-permute-start.9
  109.2 10.3 %all-to-all-done.2 = bf16[4,128,1024]{2,1,0:T(8,128)(2,1)} async-done(((bf16[4,128,1024]{2,1,0:T(8,128)(2,1)}), bf16[4,128,1024]{2,1,0:T(8,128)(2,1)}, u32[]{:S(2)}, u32[]{:S(2)}) %all-to-all-start.2) | async-done | bytes 1048608 | tf_op jit(solution)/shard_map/all_to_all | solution.py:360
  119.5 1.3 %slice_bitcast_fusion.3 = (bf16[128,1024]{1,0:T(8,128)(2,1)S(1)}, bf16[128,1024]{1,0:T(8,128)(2,1)S(1)}, bf16[128,1024]{1,0:T(8,128)(2,1)S(1)}, bf16[128,1024]{1,0:T(8,128)(2,1)S(1)}) fusion(bf16[4,128,1024]{2,1,0:T(8,128)(2,1)} %all-to-all-done.2), kind=kLoop, calls=%fused_computation.5 | loop fusion | bytes 2097152 | tf_op jit(solution)/shard_map/squeeze | solution.py:405
  120.8 1.0 maximum_bitcast_fusion
  (66 shorter events, 3.5 us)
Async XLA Ops:
  0.6 22.9 %copy-start.14 = (bf16[1,1,128,4096]{3,2,1,0:T(8,128)(2,1)S(1)}, bf16[1,1,128,4096]{3,2,1,0:T(8,128)(2,1)}, u32[]{:S(2)}) copy-start(bf16[1,1,128,4096]{3,2,1,0:T(8,128)(2,1)} %param.11) | copy-start | bytes 3145732
  0.6 21.3 %copy-start.16 = (s32[2,1,2]{2,1,0:T(1,128)S(1)}, s32[2,1,2]{2,1,0:T(1,128)}, u32[]{:S(2)}) copy-start(s32[2,1,2]{2,1,0:T(1,128)} %param.14) | copy-start | bytes 52
  0.7 22.0 %copy-start.17 = (s32[2,1,16]{2,1,0:T(1,128)S(1)}, s32[2,1,16]{2,1,0:T(1,128)}, u32[]{:S(2)}) copy-start(s32[2,1,16]{2,1,0:T(1,128)} %param.15) | copy-start | bytes 388
  0.7 22.7 %copy-start.18 = (s32[1,1,16]{2,1,0:T(1,128)S(1)}, s32[1,1,16]{2,1,0:T(1,128)}, u32[]{:S(2)}) copy-start(s32[1,1,16]{2,1,0:T(1,128)} %param.18) | copy-start | bytes 196
  15.5 15.8 %collective-permute-start.1 = (bf16[4,2,128,256]{3,2,1,0:T(8,128)(2,1)S(1)}, bf16[4,2,128,256]{3,2,1,0:T(8,128)(2,1)S(1)}, u32[]{:S(2)}, u32[]{:S(2)}) collective-permute-start(bf16[4,2,128,256]{3,2,1,0:T(8,128)(2,1)S(1)} %all_to_all.15.refs_0_), channel_id=1, source_target_pairs={{0,7},{1,0},{2,1},{3,2},{4,3},{5,4},{6,5},{7,6},{8,15},{9,8},{10,9... | collective-permute-start | bytes 1572872 | tf_op jit(solution)/shard_map/ppermute | solution.py:340
  21.4 13.4 %collective-permute-start = (bf16[4,2,128,256]{3,2,1,0:T(8,128)(2,1)S(1)}, bf16[4,2,128,256]{3,2,1,0:T(8,128)(2,1)S(1)}, u32[]{:S(2)}, u32[]{:S(2)}) collective-permute-start(bf16[4,2,128,256]{3,2,1,0:T(8,128)(2,1)S(1)} %all_to_all.15.refs_0_), channel_id=1, source_target_pairs={{0,1},{1,2},{2,3},{3,4},{4,5},{5,6},{6,7},{7,0},{8,9},{9,10},{10,1... | collective-permute-start | bytes 1572872 | tf_op jit(solution)/shard_map/ppermute | solution.py:340
  23.6 18.0 %copy-start.12 = (bf16[1,1,4,4,128]{4,3,2,1,0:T(4,128)(2,1)S(1)}, bf16[1,1,4,4,128]{4,3,2,1,0:T(4,128)(2,1)}, u32[]{:S(2)}) copy-start(bf16[1,1,4,4,128]{4,3,2,1,0:T(4,128)(2,1)} %param.21) | copy-start | bytes 12292
  23.6 18.0 %copy-start.13 = (bf16[1,1,4,4,128]{4,3,2,1,0:T(4,128)(2,1)S(1)}, bf16[1,1,4,4,128]{4,3,2,1,0:T(4,128)(2,1)}, u32[]{:S(2)}) copy-start(bf16[1,1,4,4,128]{4,3,2,1,0:T(4,128)(2,1)} %param.20) | copy-start | bytes 12292
  23.6 18.0 %copy-start.15 = (bf16[1,1,4,4,512]{4,3,2,1,0:T(4,128)(2,1)S(1)}, bf16[1,1,4,4,512]{4,3,2,1,0:T(4,128)(2,1)}, u32[]{:S(2)}) copy-start(bf16[1,1,4,4,512]{4,3,2,1,0:T(4,128)(2,1)} %param.19) | copy-start | bytes 49156
  31.4 22.6 %copy-start.4 = (bf16[4,2,128,256]{3,2,1,0:T(8,128)(2,1)}, bf16[4,2,128,256]{3,2,1,0:T(8,128)(2,1)S(1)}, u32[]{:S(2)}) copy-start(bf16[4,2,128,256]{3,2,1,0:T(8,128)(2,1)S(1)} %collective-permute-done.1.refs_2_) | copy-start | bytes 1572868
  34.8 15.0 %copy-start.6 = (bf16[4,2,128,256]{3,2,1,0:T(8,128)(2,1)}, bf16[4,2,128,256]{3,2,1,0:T(8,128)(2,1)S(1)}, u32[]{:S(2)}) copy-start(bf16[4,2,128,256]{3,2,1,0:T(8,128)(2,1)S(1)} %collective-permute-done.refs_1_) | copy-start | bytes 1572868
  34.8 15.0 %collective-permute-start.2 = (bf16[4,2,128,256]{3,2,1,0:T(8,128)(2,1)S(1)}, bf16[4,2,128,256]{3,2,1,0:T(8,128)(2,1)}, u32[]{:S(2)}, u32[]{:S(2)}) collective-permute-start(bf16[4,2,128,256]{3,2,1,0:T(8,128)(2,1)S(1)} %collective-permute-done.refs_1_), channel_id=1, source_target_pairs={{0,1},{1,2},{2,3},{3,4},{4,5},{5,6},{6,7},{7,0},{8,9},{9,10},{10,1... | collective-permute-start | bytes 1572872 | tf_op jit(solution)/shard_map/ppermute | solution.py:340
  34.8 15.0 %collective-permute-start.3 = (bf16[4,2,128,256]{3,2,1,0:T(8,128)(2,1)S(1)}, bf16[4,2,128,256]{3,2,1,0:T(8,128)(2,1)S(1)}, u32[]{:S(2)}, u32[]{:S(2)}) collective-permute-start(bf16[4,2,128,256]{3,2,1,0:T(8,128)(2,1)S(1)} %collective-permute-done.1.refs_2_), channel_id=1, source_target_pairs={{0,7},{1,0},{2,1},{3,2},{4,3},{5,4},{6,5},{7,6},{8,15},{9,8},{10,9... | collective-permute-start | bytes 1572872 | tf_op jit(solution)/shard_map/ppermute | solution.py:340
  38.0 15.9 %all-to-all-start.1 = ((bf16[4,128,1024]{2,1,0:T(8,128)(2,1)}), bf16[4,128,1024]{2,1,0:T(8,128)(2,1)S(1)}, u32[]{:S(2)}, u32[]{:S(2)}) async-start(bf16[4,128,1024]{2,1,0:T(8,128)(2,1)} %pad_maximum_fusion), calls=%async_computation.1 | async-start | bytes 2097152 | tf_op jit(solution)/shard_map/all_to_all | solution.py:360
  41.6 8.1 %collective-permute-start.4 = (bf16[4,4,768]{2,1,0:T(4,128)(2,1)S(1)}, bf16[4,4,768]{2,1,0:T(4,128)(2,1)S(1)}, u32[]{:S(2)}, u32[]{:S(2)}) collective-permute-start(bf16[4,4,768]{2,1,0:T(4,128)(2,1)S(1)} %pad_maximum_fusion.1), channel_id=1, source_target_pairs={{0,128},{128,0},{1,129},{129,1},{2,130},{130,2},{3,131},{131,3},{4... | collective-permute-start | bytes 73736 | tf_op jit(solution)/shard_map/ppermute | solution.py:387
  41.7 2.2 %copy-start = (bf16[1,1,4,4096,128]{4,3,2,1,0:T(8,128)(2,1)S(1)}, bf16[1,1,4,4096,128]{4,3,2,1,0:T(8,128)(2,1)}, u32[]{:S(2)}) copy-start(bf16[1,1,4,4096,128]{4,3,2,1,0:T(8,128)(2,1)} %param.16) | copy-start | bytes 12582916
  43.9 2.2 %copy-start.1 = (bf16[1,1,4,4096,128]{4,3,2,1,0:T(8,128)(2,1)S(1)}, bf16[1,1,4,4096,128]{4,3,2,1,0:T(8,128)(2,1)}, u32[]{:S(2)}) copy-start(bf16[1,1,4,4096,128]{4,3,2,1,0:T(8,128)(2,1)} %param.17) | copy-start | bytes 12582916
  49.8 0.8 copy-start.9
  50.6 24.6 %collective-permute-start.5 = (bf16[4,2,128,256]{3,2,1,0:T(8,128)(2,1)}, bf16[4,2,128,256]{3,2,1,0:T(8,128)(2,1)S(1)}, u32[]{:S(2)}, u32[]{:S(2)}) collective-permute-start(bf16[4,2,128,256]{3,2,1,0:T(8,128)(2,1)} %collective-permute-done.2.refs_3_), channel_id=1, source_target_pairs={{0,1},{1,2},{2,3},{3,4},{4,5},{5,6},{6,7},{7,0},{8,9},{9,10},{10,1... | collective-permute-start | bytes 1572872 | tf_op jit(solution)/shard_map/ppermute | solution.py:340
  50.6 24.6 %collective-permute-start.6 = (bf16[4,2,128,256]{3,2,1,0:T(8,128)(2,1)}, bf16[4,2,128,256]{3,2,1,0:T(8,128)(2,1)S(1)}, u32[]{:S(2)}, u32[]{:S(2)}) collective-permute-start(bf16[4,2,128,256]{3,2,1,0:T(8,128)(2,1)} %copy-done.9), channel_id=1, source_target_pairs={{0,7},{1,0},{2,1},{3,2},{4,3},{5,4},{6,5},{7,6},{8,15},{9,8},{10,9... | collective-permute-start | bytes 1572872 | tf_op jit(solution)/shard_map/ppermute | solution.py:340
  53.9 1.0 copy-start.7
  55.0 1.0 copy-start.10
  73.8 1.3 %copy-start.2 = (f32[8,512,128]{2,1,0:T(8,128)}, f32[8,512,128]{2,1,0:T(8,128)S(1)}, u32[]{:S(2)}) copy-start(f32[8,512,128]{2,1,0:T(8,128)S(1)} %get-tuple-element.32.refs_5_) | copy-start | bytes 6291460
  76.6 8.5 %collective-permute-start.8 = (bf16[2,2,128,256]{3,2,1,0:T(8,128)(2,1)}, bf16[2,2,128,256]{3,2,1,0:T(8,128)(2,1)S(1)}, u32[]{:S(2)}, u32[]{:S(2)}) collective-permute-start(bf16[2,2,128,256]{3,2,1,0:T(8,128)(2,1)} %slice.109), channel_id=1, source_target_pairs={{0,7},{1,0},{2,1},{3,2},{4,3},{5,4},{6,5},{7,6},{8,15},{9,8},{10,9... | collective-permute-start | bytes 786440 | tf_op jit(solution)/shard_map/ppermute | solution.py:340
  76.6 9.7 %collective-permute-start.7 = (bf16[2,2,128,256]{3,2,1,0:T(8,128)(2,1)}, bf16[2,2,128,256]{3,2,1,0:T(8,128)(2,1)S(1)}, u32[]{:S(2)}, u32[]{:S(2)}) collective-permute-start(bf16[2,2,128,256]{3,2,1,0:T(8,128)(2,1)} %slice.108), channel_id=1, source_target_pairs={{0,1},{1,2},{2,3},{3,4},{4,5},{5,6},{6,7},{7,0},{8,9},{9,10},{10,1... | collective-permute-start | bytes 786440 | tf_op jit(solution)/shard_map/ppermute | solution.py:340
  86.3 1.6 %copy-start.3 = (f32[8,512,128]{2,1,0:T(8,128)S(1)}, f32[8,512,128]{2,1,0:T(8,128)}, u32[]{:S(2)}) copy-start(f32[8,512,128]{2,1,0:T(8,128)} %copy-done.2) | copy-start | bytes 6291460
  98.4 4.6 %copy-start.5 = (bf16[4,2,128,256]{3,2,1,0:T(8,128)(2,1)S(1)}, bf16[4,2,128,256]{3,2,1,0:T(8,128)(2,1)}, u32[]{:S(2)}) copy-start(bf16[4,2,128,256]{3,2,1,0:T(8,128)(2,1)} %copy-done.4) | copy-start | bytes 1572868
  98.4 4.6 %copy-start.8 = (bf16[4,2,128,256]{3,2,1,0:T(8,128)(2,1)S(1)}, bf16[4,2,128,256]{3,2,1,0:T(8,128)(2,1)}, u32[]{:S(2)}) copy-start(bf16[4,2,128,256]{3,2,1,0:T(8,128)(2,1)} %copy-done.6) | copy-start | bytes 1572868
  98.4 21.1 %all-to-all-start.2 = ((bf16[4,128,1024]{2,1,0:T(8,128)(2,1)}), bf16[4,128,1024]{2,1,0:T(8,128)(2,1)}, u32[]{:S(2)}, u32[]{:S(2)}) async-start(bf16[4,128,1024]{2,1,0:T(8,128)(2,1)} %prefill_end.1), calls=%async_computation.2 | async-start | bytes 2097152 | tf_op jit(solution)/shard_map/all_to_all | solution.py:360
  103.0 1.0 copy-start.11
  106.7 1.8 %collective-permute-start.9 = (bf16[4,16,128]{2,1,0:T(8,128)(2,1)S(1)}, bf16[4,16,128]{2,1,0:T(8,128)(2,1)S(1)}, u32[]{:S(2)}, u32[]{:S(2)}) collective-permute-start(bf16[4,16,128]{2,1,0:T(8,128)(2,1)S(1)} %decode_taken.1), channel_id=1, source_target_pairs={{0,128},{128,0},{1,129},{129,1},{2,130},{130,2},{3,131},{131,3},{4... | collective-permute-start | bytes 49160 | tf_op jit(solution)/shard_map/ppermute | solution.py:406

commit v2 on v1

--- a/solution.py
+++ b/solution.py
@@ -37,6 +37,33 @@
     return lax.dot_general(a, b, (((1,), (0,)), ((), ())), preferred_element_type=jnp.float32)
 
 
+def move_kernel(plan, *refs):
+    *ins, out, sems = refs
+    copies = [
+        pltpu.make_async_copy(ins[which].at[source], out.at[target], sems.at[i])
+        for i, (which, source, target) in enumerate(plan)
+    ]
+    for copy in copies:
+        copy.start()
+    for copy in copies:
+        copy.wait()
+
+
+def move(ins, shape, plan, name):
+    space = pl.BlockSpec(memory_space=pl.ANY)
+    size = 2 * math.prod(shape)
+    return pl.pallas_call(
+        functools.partial(move_kernel, plan),
+        in_specs=[space] * len(ins),
+        out_specs=space,
+        out_shape=jax.ShapeDtypeStruct(shape, ins[0].dtype),
+        scratch_shapes=[pltpu.SemaphoreType.DMA((len(plan),))],
+        compiler_params=pltpu.CompilerParams(vmem_limit_bytes=1 << 20),
+        cost_estimate=pl.CostEstimate(flops=0, bytes_accessed=2 * size, transcendentals=0),
+        name=name,
+    )(*ins)
+
+
 SAFE = 1e30
 
 
@@ -47,7 +74,7 @@
     sources = [(z + d) % NZ for d in offsets]
     lanes = [slice(g * HD, (g + 1) * HD) for g in range(n)]
     heads = [slice(a * ROWS, (a + 1) * ROWS) for a in range(RATIO)]
-    *refs, m_ref, l_ref = refs
+    *refs, m_ref, l_ref, worst = refs
     if start:
         *kvs, rows_out, acc_out = refs
     elif not last:
@@ -56,18 +83,21 @@
         *kvs, low_half, high_half, rows_in, acc_in, out_ref, acc_end = refs
 
     def keys_values(h, c):
-        def one(kv, at):
-            return kv[pl.ds(at, 1), h].reshape(ROWS, 2 * HD)
-
-        blocks = [one(kv, c) for kv in kvs]
-        if last:
-            half = NX // 2
-            blocks.append(jnp.where(c < half, *[one(kv, c % half) for kv in (low_half, high_half)]))
-        k = jnp.concatenate([b[:, :HD] for b in blocks], axis=0)
-        v = jnp.concatenate([b[:, HD:] for b in blocks], axis=0)
-        return k, v
-
-    def block(x, carry):
+        both = []
+        for part in range(2):
+
+            def one(kv, at):
+                return kv[pl.ds(at, 1), part, :, h * HD : (h + 1) * HD].reshape(ROWS, HD)
+
+            blocks = [one(kv, c) for kv in kvs]
+            if last:
+                half = NX // 2
+                pair = [one(kv, c % half) for kv in (low_half, high_half)]
+                blocks.append(jnp.where(c < half, *pair))
+            both.append(jnp.concatenate(blocks, axis=0))
+        return both
+
+    def block(x, quickly):
         row0 = x * XROWS + z * ROWS
         low = jnp.where(row0 >= first, first // XROWS, 0)
         qx = q_ref[pl.ds(x, 1)].reshape(ROWS, HEADS * RATIO * HD)
@@ -157,12 +187,10 @@
 
         end = x if start else x + 1
         begin()
-        lax.fori_loop(low, end, quick_step, 0)
-
-        @pl.when(jnp.logical_not(jnp.max(l_ref[...]) < SAFE))
-        def _():
-            begin()
-            lax.fori_loop(low, end, careful_step, 0)
+        lax.fori_loop(low, end, quick_step if quickly else careful_step, 0)
+        if quickly:
+            tiles = [ls[h][8 * i : 8 * i + 8] for h in range(HEADS) for i in range(RATIO * ROWS // 8)]
+            worst[...] = functools.reduce(jnp.maximum, tiles, worst[...])
 
         for h in range(HEADS):
             if last:
@@ -175,9 +203,20 @@
                 total = jnp.sum(ls[h][...].T, axis=0, keepdims=True)
                 line = lax.broadcasted_iota(jnp.int32, (8, RATIO * ROWS), 0)
                 rows_out[pl.ds(spots[h], 1)] = jnp.where(line == 0, top, total)[None]
-        return carry
-
-    lax.fori_loop(0, NX, block, 0)
+
+    def blocks(quickly):
+        def one(x, carry):
+            block(x, quickly)
+            return carry
+
+        lax.fori_loop(0, NX, one, 0)
+
+    worst[...] = jnp.zeros(worst.shape, jnp.float32)
+    blocks(True)
+
+    @pl.when(jnp.logical_not(jnp.max(worst[...]) < SAFE))
+    def _():
+        blocks(False)
 
 
 def stage(ints, q, offsets, shards, ends=(), state=()):
@@ -198,7 +237,7 @@
         grid=(1,),
         in_specs=[whole(a) for a in (q, *shards, *ends, *state)],
         out_specs=whole(q) if last else [whole(a) for a in held],
-        scratch_shapes=[tile] * (3 if last else 2),
+        scratch_shapes=[tile] * (3 if last else 2) + [pltpu.VMEM((8, HD), jnp.float32)],
     )
     pairs = 7 * HEADS * rows * ROWS * len(offsets)
     return pl.pallas_call(
@@ -232,33 +271,41 @@
     return mine & (key % STEPS <= row // RATIO % STEPS)
 
 
-def cached_kernel(ints, q_ref, kn_ref, vn_ref, k_ref, v_ref, out_ref):
-    n = pl.program_id(0)
-    slot = ints[I_CTX] * NEW % SLOTS + n
-    length = ints[I_LEN + slot]
-    q = q_ref[0]
-    ok = lax.broadcasted_iota(jnp.int32, (q.shape[0], k_ref.shape[1]), 1) < length
-    out_ref[0] = attend(q, [(k_ref[0], v_ref[0], ok), (kn_ref[0], vn_ref[0], fresh_ok(1))])
-
-
-def decode_cached(ints, q, k_new, v_new, cache_k, cache_v):
+def cached_kernel(ints, q_ref, kn_ref, vn_ref, k_ref, v_ref, after_ref, out_ref, keys, values, sems):
+    rows = q_ref.shape[0]
+    pairs = [(k_ref, keys), (v_ref, values)]
+    copies = [
+        [pltpu.make_async_copy(src.at[n], dst.at[n], sems.at[i, n]) for i, (src, dst) in enumerate(pairs)]
+        for n in range(rows)
+    ]
+    for pair in copies:
+        for copy in pair:
+            copy.start()
+    slot0 = ints[I_CTX] * NEW % SLOTS
+    for n, pair in enumerate(copies):
+        q = q_ref[n]
+        length = ints[I_LEN + slot0 + n]
+        ok = lax.broadcasted_iota(jnp.int32, (q.shape[0], keys.shape[1]), 1) < length
+        for copy in pair:
+            copy.wait()
+        out_ref[n] = attend(q, [(keys[n], values[n], ok), (kn_ref[n], vn_ref[n], fresh_ok(1))])
+
+
+def decode_cached(ints, q, k_new, v_new, cache_k, cache_v, after):
     rows, context, _ = cache_k.shape
     n = q.shape[1]
 
-    def whole(shape):
-        return pl.BlockSpec((1,) + shape, lambda i, s: (i, 0, 0))
-
+    def whole(array):
+        return pl.BlockSpec(array.shape, lambda i, s: (0, 0, 0))
+
+    far = pl.BlockSpec(memory_space=pltpu.HBM)
     grid = pltpu.PrefetchScalarGridSpec(
         num_scalar_prefetch=1,
-        grid=(rows,),
-        in_specs=[
-            whole((n, HD)),
-            whole((STEPS, HD)),
-            whole((STEPS, HD)),
-            whole((context, HD)),
-            whole((context, HD)),
-        ],
-        out_specs=whole((n, HD)),
+        grid=(1,),
+        in_specs=[whole(q), whole(k_new), whole(v_new), far, far, pl.BlockSpec(memory_space=pl.ANY)],
+        out_specs=whole(q),
+        scratch_shapes=[pltpu.VMEM(cache_k.shape, cache_k.dtype)] * 2
+        + [pltpu.SemaphoreType.DMA((2, rows))],
     )
     return pl.pallas_call(
         cached_kernel,
@@ -271,7 +318,7 @@
             transcendentals=rows * context * n,
         ),
         name="decode_cached",
-    )(ints, q, k_new, v_new, cache_k, cache_v)
+    )(ints, q, k_new, v_new, cache_k, cache_v, after)
 
 
 def taken_kernel(offsets, ints, q_ref, kn_ref, vn_ref, *refs):
@@ -297,8 +344,8 @@
     parts = []
     for d, kv in zip(offsets, [kv[...] for kv in kvs] + [tail]):
         token = col + (z + d) % NZ * ROWS
-        kv = kv.reshape(width, 2 * HD)
-        parts.append((kv[:, :HD], kv[:, HD:], (token >= begin) & (token < stop)))
+        k, v = kv[:, 0].reshape(width, HD), kv[:, 1].reshape(width, HD)
+        parts.append((k, v, (token >= begin) & (token < stop)))
     kn, vn = [r[...].reshape(rows * STEPS, HD) for r in (kn_ref, vn_ref)]
     out = attend(q, parts + [(kn, vn, fresh_ok(rows))])
     out_ref[...] = out.reshape(out_ref.shape)
@@ -307,8 +354,7 @@
 def decode_taken(ints, q, k_new, v_new, shards, ends, offsets):
     def one_head(array):
         return pl.BlockSpec(
-            (array.shape[0], pl.squeezed, ROWS, 2 * HD),
-            lambda i, s: (0, s[I_CTX] % NZ // NEW, 0, 0),
+            (array.shape[0], 2, ROWS, HD), lambda i, s: (0, 0, 0, s[I_CTX] % NZ // NEW)
         )
 
     def whole(array):
@@ -361,48 +407,47 @@
 
     k, v, q = k_pf[0, 0], v_pf[0, 0], q_pf[0, 0]
 
-    def cols(array, head):
-        return array[:, head * HD : (head + 1) * HD]
-
-    packed = jnp.stack(
-        [
-            jnp.concatenate([cols(a, HEADS * x + h) for a in (k, v)], axis=1)
-            for x in range(NX)
-            for h in range(HEADS)
-        ]
-    ).reshape(NX, HEADS, ROWS, 2 * HD)
+    everything = slice(None)
+
+    def share(x, width):
+        return everything, pl.ds(x * width, width)
+
+    kv_width = HEADS * HD
+    plan = [(part, share(x, kv_width), (x, part)) for x in range(NX) for part in range(2)]
+    packed = move((k, v), (NX, 2, ROWS, kv_width), plan, "pack_kv")
     own_kv = along_x(packed)
-    q, own_kv = together((q, own_kv))
-    width = HEADS * RATIO * HD
-    queries = jnp.stack([q[:, x * width : (x + 1) * width] for x in range(NX)])
-
-    up1, down1 = along_z(own_kv, 1), along_z(own_kv, -1)
-    up1, down1, queries, ints = together((up1, down1, queries, ints))
-    up2, down2 = along_z(up1, 1), along_z(down1, -1)
-    queries = along_x(queries)
     qd, kn, vn = q_dec[0, 0], k_new[0, 0], v_new[0, 0]
     rows = qd.shape[0]
     lists = (rows, STEPS * RATIO, HD)
-    own = decode_cached(ints, qd.reshape(lists), kn, vn, cache_k[0, 0], cache_v[0, 0])
+    own_kv, ints, q = together((own_kv, ints, q))
+    width = HEADS * RATIO * HD
+    plan = [(0, share(x, width), (x,)) for x in range(NX)]
+    queries = along_x(move((q,), (NX, ROWS, width), plan, "pack_q"))
+
+    up1, down1 = along_z(own_kv, 1), along_z(own_kv, -1)
     fresh = lax.ppermute(jnp.concatenate([qd, kn, vn], axis=-1), "section", swap)
-    up2, down2, own, fresh = together((up2, down2, own, fresh))
+    their_q = fresh[..., : RATIO * HD].reshape(lists)
+    their_k = fresh[..., RATIO * HD : (RATIO + 1) * HD]
+    their_v = fresh[..., (RATIO + 1) * HD :]
+    up1, down1, their_q, their_k, their_v = together((up1, down1, their_q, their_k, their_v))
+    up2, down2 = along_z(up1, 1), along_z(down1, -1)
+    own = decode_cached(ints, qd.reshape(lists), kn, vn, cache_k[0, 0], cache_v[0, 0], up1)
+    up2, down2, queries, own = together((up2, down2, queries, own))
     up3, down3 = along_z(up2, 1), along_z(down2, -1)
-    near, near_at = [own_kv, up1, down1, up2, down2], [0, -1, 1, -2, 2]
+    near, near_at = [own_kv, up1, down1, up2], [0, -1, 1, -2]
     lines, acc = stage(ints, queries, near_at, near)
     up3, down3, lines = together((up3, down3, lines))
     ends = [along_z(up3[: NX // 2], 1), along_z(down3[NX // 2 :], -1)]
-    far, far_at, end_at = [up3, down3], [-3, 3], [4]
-    out = stage(ints, queries, far_at + end_at, far, ends, (lines, acc))
-
-    their_q = fresh[..., : RATIO * HD].reshape(lists)
-    their_k = fresh[..., RATIO * HD : (RATIO + 1) * HD]
-    their_v = fresh[..., (RATIO + 1) * HD :]
+    far, far_at = [down2, up3, down3], [2, -3, 3, 4]
+    out = stage(ints, queries, far_at, far, ends, (lines, acc))
+
     their_q, out = together((their_q, out))
     theirs = decode_taken(
-        ints, their_q, their_k, their_v, near + far, ends, near_at + far_at + end_at
+        ints, their_q, their_k, their_v, near + far, ends, near_at + far_at
     )
     out = along_x(out)
-    pf_result = jnp.concatenate([out[x] for x in range(NX)], axis=1)
+    plan = [(0, (x,), share(x, width)) for x in range(NX)]
+    pf_result = move((out,), q.shape, plan, "assemble")
     back = lax.ppermute(theirs, "section", swap)
     slots = (ctx * rows) % SLOTS + jnp.arange(rows, dtype=jnp.int32)
     taken = slot_order[1 - section, 0, :2]

time: 122 us -> 114 us (0.934)
  the two profiles are of different devices: /device:TPU:8 before, /device:TPU:16 now
where the time goes in v2:
time: 114 us; the launch traced here: 113 us
  Pallas kernels  41.1 us (36%)
  waiting for transfers between devices  26.1 us (23%)
  starting transfers between devices  24.9 us (22%)
  local copies, waits for them, and re-layouts  17.3 us (15%)
  other arithmetic  3.01 us (3%)
    pallas_call x2, Pallas kernels, stage(): pl.pallas_call(functools.partial(stage_kernel, offsets, start, last), gri...  31.2 us
    unnamed x37, local copies, waits for them, and re-layouts  15.7 us
    ppermute x8, waiting for transfers between devices, along_z(): return lax.ppermute(value, 'ctx', pairs)  13.3 us
    all_to_all x3, starting transfers between devices, along_x(): lax.all_to_all(value, 'ctx', 0, 0, axis_index_groups=ALONG_X, tiled=True)  12.7 us
    ppermute x8, starting transfers between devices, along_z(): return lax.ppermute(value, 'ctx', pairs)  12 us
    all_to_all x3, waiting for transfers between devices, along_x(): lax.all_to_all(value, 'ctx', 0, 0, axis_index_groups=ALONG_X, tiled=True)  10.6 us
    pallas_call x1, Pallas kernels, decode_cached(): pl.pallas_call(cached_kernel, grid_spec=grid, out_shape=jax.ShapeDtypeStr...  4.3 us
    pallas_call x3, Pallas kernels, move(): pl.pallas_call(functools.partial(move_kernel, plan), in_specs=[space] * l...  2.83 us
  transfers between devices with their start and end apart: 13, of which 10 were waited for; matrix products, arithmetic and copies ran while one was open for 5% of the time, Pallas kernels for 25%

profile of v2, /device:TPU:16, one launch (start us, length us, event | category | flops | bytes accessed | tf_op | source)
XLA Modules:
  0.0 113.4 jit_solution(12170738772886671769)
XLA Ops:
  3.4 4.3 %all-to-all-start = ((bf16[4,2,128,256]{3,2,1,0:T(8,128)(2,1)}), bf16[4,2,128,256]{3,2,1,0:T(8,128)(2,1)S(1)}, u32[]{:S(2)}, u32[]{:S(2)}) async-start(bf16[4,2,128,256]{3,2,1,0:T(8,128)(2,1)} %pack_kv.1), calls=%async_computation | async-start | bytes 1048576 | tf_op jit(solution)/shard_map/all_to_all | solution.py:406
  8.3 1.4 %reduce.6 = s32[2,2]{1,0:T(2,128)S(1)} reduce(s32[2,1,2]{2,1,0:T(1,128)} %param.14, s32[]{:T(128)} %broadcast.12), dimensions={1}, to_apply=%param.14.reduce_sub_computation.3 | reduce | bytes 36 | tf_op args[3]
  9.7 1.4 %reduce.7 = s32[2,16]{1,0:T(2,128)S(1)} reduce(s32[2,1,16]{2,1,0:T(1,128)} %param.15, s32[]{:T(128)} %broadcast.12), dimensions={1}, to_apply=%param.15.reduce_sub_computation.3 | reduce | bytes 260 | tf_op args[4]
  11.9 5.3 %all-to-all-done.refs_0_ = bf16[4,2,128,256]{3,2,1,0:T(8,128)(2,1)S(1)} async-done(((bf16[4,2,128,256]{3,2,1,0:T(8,128)(2,1)}), bf16[4,2,128,256]{3,2,1,0:T(8,128)(2,1)S(1)}, u32[]{:S(2)}, u32[]{:S(2)}) %all-to-all-start) | async-done | bytes 524320 | tf_op jit(solution)/shard_map/all_to_all | solution.py:406
  17.2 5.9 %collective-permute-start.1 = (bf16[4,2,128,256]{3,2,1,0:T(8,128)(2,1)S(1)}, bf16[4,2,128,256]{3,2,1,0:T(8,128)(2,1)S(1)}, u32[]{:S(2)}, u32[]{:S(2)}) collective-permute-start(bf16[4,2,128,256]{3,2,1,0:T(8,128)(2,1)S(1)} %all-to-all-done.refs_0_), channel_id=1, source_target_pairs={{0,7},{1,0},{2,1},{3,2},{4,3},{5,4},{6,5},{7,6},{8,15},{9,8},{10,9... | collective-permute-start | bytes 1572872 | tf_op jit(solution)/shard_map/ppermute | solution.py:386
  23.0 1.2 %copy-done.2 = bf16[1,1,128,4096]{3,2,1,0:T(8,128)(2,1)S(1)} copy-done((bf16[1,1,128,4096]{3,2,1,0:T(8,128)(2,1)S(1)}, bf16[1,1,128,4096]{3,2,1,0:T(8,128)(2,1)}, u32[]{:S(2)}) %copy-start.2) | copy-done | bytes 1048600
  24.3 1.0 pack_q.1
  25.3 3.5 %all-to-all-start.1 = ((bf16[4,128,1024]{2,1,0:T(8,128)(2,1)}), bf16[4,128,1024]{2,1,0:T(8,128)(2,1)S(1)}, u32[]{:S(2)}, u32[]{:S(2)}) async-start(bf16[4,128,1024]{2,1,0:T(8,128)(2,1)} %pack_q.1), calls=%async_computation.1 | async-start | bytes 2097152 | tf_op jit(solution)/shard_map/all_to_all | solution.py:406
  29.0 1.2 %collective-permute-done.2 = bf16[4,4,768]{2,1,0:T(4,128)(2,1)S(1)} collective-permute-done((bf16[4,4,768]{2,1,0:T(4,128)(2,1)S(1)}, bf16[4,4,768]{2,1,0:T(4,128)(2,1)S(1)}, u32[]{:S(2)}, u32[]{:S(2)}) %collective-permute-start.2) | collective-permute-done | bytes 24608 | tf_op jit(solution)/shard_map/ppermute | solution.py:428
  30.2 2.5 %collective-permute-done.1.refs_2_ = bf16[4,2,128,256]{3,2,1,0:T(8,128)(2,1)S(1)} collective-permute-done((bf16[4,2,128,256]{3,2,1,0:T(8,128)(2,1)S(1)}, bf16[4,2,128,256]{3,2,1,0:T(8,128)(2,1)S(1)}, u32[]{:S(2)}, u32[]{:S(2)}) %collective-permute-start.1) | collective-permute-done | bytes 524320 | tf_op jit(solution)/shard_map/ppermute | solution.py:386
  32.7 3.4 %collective-permute-done.after_ref.refs_1_ = bf16[4,2,128,256]{3,2,1,0:T(8,128)(2,1)S(1)} collective-permute-done((bf16[4,2,128,256]{3,2,1,0:T(8,128)(2,1)S(1)}, bf16[4,2,128,256]{3,2,1,0:T(8,128)(2,1)S(1)}, u32[]{:S(2)}, u32[]{:S(2)}) %collective-permute-start) | collective-permute-done | bytes 524320 | tf_op jit(solution)/shard_map/ppermute | solution.py:386
  36.4 1.7 %collective-permute-start.3 = (bf16[4,2,128,256]{3,2,1,0:T(8,128)(2,1)S(1)}, bf16[4,2,128,256]{3,2,1,0:T(8,128)(2,1)S(1)}, u32[]{:S(2)}, u32[]{:S(2)}) collective-permute-start(bf16[4,2,128,256]{3,2,1,0:T(8,128)(2,1)S(1)} %collective-permute-done.after_ref.refs_1_), channel_id=1, source_target_pairs={{0,1},{1,2},{2,3},{3,4},{4,5},{5,6},{6,7},{7,0},{8,9},{9,10},{10,1... | collective-permute-start | bytes 1572872 | tf_op jit(solution)/shard_map/ppermute | solution.py:386
  38.2 2.2 %copy-done = bf16[1,1,4,4096,128]{4,3,2,1,0:T(8,128)(2,1)S(1)} copy-done((bf16[1,1,4,4096,128]{4,3,2,1,0:T(8,128)(2,1)S(1)}, bf16[1,1,4,4096,128]{4,3,2,1,0:T(8,128)(2,1)}, u32[]{:S(2)}) %copy-start) | copy-done | bytes 4194328
  40.4 2.2 %copy-done.1 = bf16[1,1,4,4096,128]{4,3,2,1,0:T(8,128)(2,1)S(1)} copy-done((bf16[1,1,4,4096,128]{4,3,2,1,0:T(8,128)(2,1)S(1)}, bf16[1,1,4,4096,128]{4,3,2,1,0:T(8,128)(2,1)}, u32[]{:S(2)}) %copy-start.1) | copy-done | bytes 4194328
  42.6 4.3 %decode_cached.1 = bf16[4,16,128]{2,1,0:T(8,128)(2,1)S(1)} custom-call(s32[54]{0:T(128)S(1)} %concatenate.6.ints, bf16[4,16,128]{2,1,0:T(8,128)(2,1)S(1)} %reshape_squeeze.3.q_ref, bf16[4,4,128]{2,1,0:T(4,128)(2,1)S(1)} %bitcast.22, bf16[4,4,128]{2,1,0:T(4,128)(2,1)S(1)} %bitcast.20, bf16[4,4096,128]{2,1,0:T(8,128)(2,1)S(1)} %bitcast.14, ...), custom_call_target="tpu_custom_call" | custom-call | flops 134217728 | bytes 8388608 | tf_op jit(solution)/shard_map/decode_cached/pallas_call | solution.py:310
  47.2 1.4 %collective-permute-done.3.refs_3_ = bf16[4,2,128,256]{3,2,1,0:T(8,128)(2,1)S(1)} collective-permute-done((bf16[4,2,128,256]{3,2,1,0:T(8,128)(2,1)S(1)}, bf16[4,2,128,256]{3,2,1,0:T(8,128)(2,1)S(1)}, u32[]{:S(2)}, u32[]{:S(2)}) %collective-permute-start.3) | collective-permute-done | bytes 524320 | tf_op jit(solution)/shard_map/ppermute | solution.py:386
  49.8 1.6 %collective-permute-start.5 = (bf16[4,2,128,256]{3,2,1,0:T(8,128)(2,1)}, bf16[4,2,128,256]{3,2,1,0:T(8,128)(2,1)S(1)}, u32[]{:S(2)}, u32[]{:S(2)}) collective-permute-start(bf16[4,2,128,256]{3,2,1,0:T(8,128)(2,1)} %copy-done.7), channel_id=1, source_target_pairs={{0,1},{1,2},{2,3},{3,4},{4,5},{5,6},{6,7},{7,0},{8,9},{9,10},{10,1... | collective-permute-start | bytes 1572872 | tf_op jit(solution)/shard_map/ppermute | solution.py:386
  51.4 1.0 copy-done.5
  52.5 1.0 copy-done.8
  53.5 20.1 %prefill_begin.1 = (f32[8,8,512]{2,1,0:T(8,128)S(1)}, f32[8,512,128]{2,1,0:T(8,128)S(1)}) custom-call(s32[54]{0:T(128)S(1)} %concatenate.6.ints, bf16[4,128,1024]{2,1,0:T(8,128)(2,1)S(1)} %all-to-all-done.1.q_ref, bf16[4,2,128,256]{3,2,1,0:T(8,128)(2,1)S(1)} %all-to-all-done.refs_0_, bf16[4,2,128,256]{3,2,1,0:T(8,128)(2,1)S(1)} %collective-permute-done.after_ref.refs_1_, ...), custom_call_target="tpu_custom_call" | custom-call | flops 1879048192 | bytes 8388608 | tf_op jit(solution)/shard_map/prefill_begin/pallas_call | solution.py:243
  73.8 2.0 %collective-permute-start.7 = (bf16[2,2,128,256]{3,2,1,0:T(8,128)(2,1)S(1)}, bf16[2,2,128,256]{3,2,1,0:T(8,128)(2,1)S(1)}, u32[]{:S(2)}, u32[]{:S(2)}) collective-permute-start(bf16[2,2,128,256]{3,2,1,0:T(8,128)(2,1)S(1)} %slice.18), channel_id=1, source_target_pairs={{0,1},{1,2},{2,3},{3,4},{4,5},{5,6},{6,7},{7,0},{8,9},{9,10},{10,1... | collective-permute-start | bytes 786440 | tf_op jit(solution)/shard_map/ppermute | solution.py:386
  75.9 4.3 %collective-permute-done.8.refs_4_.refs_8_ = bf16[2,2,128,256]{3,2,1,0:T(8,128)(2,1)S(1)} collective-permute-done((bf16[2,2,128,256]{3,2,1,0:T(8,128)(2,1)S(1)}, bf16[2,2,128,256]{3,2,1,0:T(8,128)(2,1)S(1)}, u32[]{:S(2)}, u32[]{:S(2)}) %collective-permute-start.8) | collective-permute-done | bytes 262176 | tf_op jit(solution)/shard_map/ppermute | solution.py:386
  80.2 1.3 %collective-permute-done.7.refs_3_.refs_7_ = bf16[2,2,128,256]{3,2,1,0:T(8,128)(2,1)S(1)} collective-permute-done((bf16[2,2,128,256]{3,2,1,0:T(8,128)(2,1)S(1)}, bf16[2,2,128,256]{3,2,1,0:T(8,128)(2,1)S(1)}, u32[]{:S(2)}, u32[]{:S(2)}) %collective-permute-start.7) | collective-permute-done | bytes 262176 | tf_op jit(solution)/shard_map/ppermute | solution.py:386
  81.5 11.1 %prefill_end.1 = bf16[4,128,1024]{2,1,0:T(8,128)(2,1)S(1)} custom-call(s32[54]{0:T(128)S(1)} %concatenate.6.ints, bf16[4,128,1024]{2,1,0:T(8,128)(2,1)S(1)} %all-to-all-done.1.q_ref, bf16[4,2,128,256]{3,2,1,0:T(8,128)(2,1)} %collective-permute-done.4.refs_0_.refs_4_, bf16[4,2,128,256]{3,2,1,0:T(8,128)(2,1)S(1)} %collective-permute-done.5.refs_1_.refs_5_, ...), custom_call_target="tpu_custom_call" | custom-call | flops 1879048192 | bytes 8388608 | tf_op jit(solution)/shard_map/prefill_end/pallas_call | solution.py:243
  92.6 1.0 copy-done.3
  94.3 4.8 %all-to-all-start.2 = ((bf16[4,128,1024]{2,1,0:T(8,128)(2,1)}), bf16[4,128,1024]{2,1,0:T(8,128)(2,1)S(1)}, u32[]{:S(2)}, u32[]{:S(2)}) async-start(bf16[4,128,1024]{2,1,0:T(8,128)(2,1)} %copy-done.3), calls=%async_computation.2 | async-start | bytes 2097152 | tf_op jit(solution)/shard_map/all_to_all | solution.py:406
  99.1 1.0 copy-done.6
  100.2 1.0 copy-done.9
  102.1 2.8 %decode_taken.1 = bf16[4,16,128]{2,1,0:T(8,128)(2,1)S(1)} custom-call(s32[54]{0:T(128)S(1)} %concatenate.6.ints, bf16[4,16,128]{2,1,0:T(8,128)(2,1)S(1)} %reshape.25.q_ref, bf16[4,4,128]{2,1,0:T(4,128)(2,1)S(1)} %get-tuple-element.37.kn_ref, bf16[4,4,128]{2,1,0:T(4,128)(2,1)S(1)} %get-tuple-element.38.vn_ref, ...), custom_call_target="tpu_custom_call" | custom-call | flops 134217728 | bytes 2097152 | tf_op jit(solution)/shard_map/decode_taken/pallas_call | solution.py:372
  105.2 1.0 collective-permute-done.9
  106.9 5.3 %all-to-all-done.2.refs_0_ = bf16[4,128,1024]{2,1,0:T(8,128)(2,1)S(1)} async-done(((bf16[4,128,1024]{2,1,0:T(8,128)(2,1)}), bf16[4,128,1024]{2,1,0:T(8,128)(2,1)S(1)}, u32[]{:S(2)}, u32[]{:S(2)}) %all-to-all-start.2) | async-done | bytes 1048608 | tf_op jit(solution)/shard_map/all_to_all | solution.py:406
  112.2 1.0 assemble.1
  (55 shorter events, 9.0 us)
Async XLA Ops:
  0.6 1.0 copy-start.12
  1.6 0.9 copy-start.13
  2.5 26.3 %copy-start.14 = (bf16[1,1,4,4,128]{4,3,2,1,0:T(4,128)(2,1)S(1)}, bf16[1,1,4,4,128]{4,3,2,1,0:T(4,128)(2,1)}, u32[]{:S(2)}) copy-start(bf16[1,1,4,4,128]{4,3,2,1,0:T(4,128)(2,1)} %param.21) | copy-start | bytes 12292
  2.5 26.3 %copy-start.15 = (bf16[1,1,4,4,128]{4,3,2,1,0:T(4,128)(2,1)S(1)}, bf16[1,1,4,4,128]{4,3,2,1,0:T(4,128)(2,1)}, u32[]{:S(2)}) copy-start(bf16[1,1,4,4,128]{4,3,2,1,0:T(4,128)(2,1)} %param.20) | copy-start | bytes 12292
  2.5 26.3 %copy-start.16 = (bf16[1,1,4,4,512]{4,3,2,1,0:T(4,128)(2,1)S(1)}, bf16[1,1,4,4,512]{4,3,2,1,0:T(4,128)(2,1)}, u32[]{:S(2)}) copy-start(bf16[1,1,4,4,512]{4,3,2,1,0:T(4,128)(2,1)} %param.19) | copy-start | bytes 49156
  3.4 13.8 %all-to-all-start = ((bf16[4,2,128,256]{3,2,1,0:T(8,128)(2,1)}), bf16[4,2,128,256]{3,2,1,0:T(8,128)(2,1)S(1)}, u32[]{:S(2)}, u32[]{:S(2)}) async-start(bf16[4,2,128,256]{3,2,1,0:T(8,128)(2,1)} %pack_kv.1), calls=%async_computation | async-start | bytes 1048576 | tf_op jit(solution)/shard_map/all_to_all | solution.py:406
  17.2 15.6 %collective-permute-start.1 = (bf16[4,2,128,256]{3,2,1,0:T(8,128)(2,1)S(1)}, bf16[4,2,128,256]{3,2,1,0:T(8,128)(2,1)S(1)}, u32[]{:S(2)}, u32[]{:S(2)}) collective-permute-start(bf16[4,2,128,256]{3,2,1,0:T(8,128)(2,1)S(1)} %all-to-all-done.refs_0_), channel_id=1, source_target_pairs={{0,7},{1,0},{2,1},{3,2},{4,3},{5,4},{6,5},{7,6},{8,15},{9,8},{10,9... | collective-permute-start | bytes 1572872 | tf_op jit(solution)/shard_map/ppermute | solution.py:386
  23.0 13.1 %collective-permute-start = (bf16[4,2,128,256]{3,2,1,0:T(8,128)(2,1)S(1)}, bf16[4,2,128,256]{3,2,1,0:T(8,128)(2,1)S(1)}, u32[]{:S(2)}, u32[]{:S(2)}) collective-permute-start(bf16[4,2,128,256]{3,2,1,0:T(8,128)(2,1)S(1)} %all-to-all-done.refs_0_), channel_id=1, source_target_pairs={{0,1},{1,2},{2,3},{3,4},{4,5},{5,6},{6,7},{7,0},{8,9},{9,10},{10,1... | collective-permute-start | bytes 1572872 | tf_op jit(solution)/shard_map/ppermute | solution.py:386
  23.0 1.2 %copy-start.2 = (bf16[1,1,128,4096]{3,2,1,0:T(8,128)(2,1)S(1)}, bf16[1,1,128,4096]{3,2,1,0:T(8,128)(2,1)}, u32[]{:S(2)}) copy-start(bf16[1,1,128,4096]{3,2,1,0:T(8,128)(2,1)} %param.11) | copy-start | bytes 3145732
  25.3 21.6 %all-to-all-start.1 = ((bf16[4,128,1024]{2,1,0:T(8,128)(2,1)}), bf16[4,128,1024]{2,1,0:T(8,128)(2,1)S(1)}, u32[]{:S(2)}, u32[]{:S(2)}) async-start(bf16[4,128,1024]{2,1,0:T(8,128)(2,1)} %pack_q.1), calls=%async_computation.1 | async-start | bytes 2097152 | tf_op jit(solution)/shard_map/all_to_all | solution.py:406
  28.9 1.3 %collective-permute-start.2 = (bf16[4,4,768]{2,1,0:T(4,128)(2,1)S(1)}, bf16[4,4,768]{2,1,0:T(4,128)(2,1)S(1)}, u32[]{:S(2)}, u32[]{:S(2)}) collective-permute-start(bf16[4,4,768]{2,1,0:T(4,128)(2,1)S(1)} %pad_maximum_fusion), channel_id=1, source_target_pairs={{0,128},{128,0},{1,129},{129,1},{2,130},{130,2},{3,131},{131,3},{4... | collective-permute-start | bytes 73736 | tf_op jit(solution)/shard_map/ppermute | solution.py:428
  32.7 14.1 %copy-start.4 = (bf16[4,2,128,256]{3,2,1,0:T(8,128)(2,1)}, bf16[4,2,128,256]{3,2,1,0:T(8,128)(2,1)S(1)}, u32[]{:S(2)}) copy-start(bf16[4,2,128,256]{3,2,1,0:T(8,128)(2,1)S(1)} %collective-permute-done.1.refs_2_) | copy-start | bytes 1572868
  36.1 11.1 %collective-permute-start.4 = (bf16[4,2,128,256]{3,2,1,0:T(8,128)(2,1)S(1)}, bf16[4,2,128,256]{3,2,1,0:T(8,128)(2,1)}, u32[]{:S(2)}, u32[]{:S(2)}) collective-permute-start(bf16[4,2,128,256]{3,2,1,0:T(8,128)(2,1)S(1)} %collective-permute-done.1.refs_2_), channel_id=1, source_target_pairs={{0,7},{1,0},{2,1},{3,2},{4,3},{5,4},{6,5},{7,6},{8,15},{9,8},{10,9... | collective-permute-start | bytes 1572872 | tf_op jit(solution)/shard_map/ppermute | solution.py:386
  36.4 12.2 %collective-permute-start.3 = (bf16[4,2,128,256]{3,2,1,0:T(8,128)(2,1)S(1)}, bf16[4,2,128,256]{3,2,1,0:T(8,128)(2,1)S(1)}, u32[]{:S(2)}, u32[]{:S(2)}) collective-permute-start(bf16[4,2,128,256]{3,2,1,0:T(8,128)(2,1)S(1)} %collective-permute-done.after_ref.refs_1_), channel_id=1, source_target_pairs={{0,1},{1,2},{2,3},{3,4},{4,5},{5,6},{6,7},{7,0},{8,9},{9,10},{10,1... | collective-permute-start | bytes 1572872 | tf_op jit(solution)/shard_map/ppermute | solution.py:386
  38.2 2.2 %copy-start = (bf16[1,1,4,4096,128]{4,3,2,1,0:T(8,128)(2,1)S(1)}, bf16[1,1,4,4096,128]{4,3,2,1,0:T(8,128)(2,1)}, u32[]{:S(2)}) copy-start(bf16[1,1,4,4096,128]{4,3,2,1,0:T(8,128)(2,1)} %param.16) | copy-start | bytes 12582916
  40.4 2.2 %copy-start.1 = (bf16[1,1,4,4096,128]{4,3,2,1,0:T(8,128)(2,1)S(1)}, bf16[1,1,4,4096,128]{4,3,2,1,0:T(8,128)(2,1)}, u32[]{:S(2)}) copy-start(bf16[1,1,4,4096,128]{4,3,2,1,0:T(8,128)(2,1)} %param.17) | copy-start | bytes 12582916
  48.6 0.8 copy-start.7
  49.4 24.3 %collective-permute-start.6 = (bf16[4,2,128,256]{3,2,1,0:T(8,128)(2,1)}, bf16[4,2,128,256]{3,2,1,0:T(8,128)(2,1)S(1)}, u32[]{:S(2)}, u32[]{:S(2)}) collective-permute-start(bf16[4,2,128,256]{3,2,1,0:T(8,128)(2,1)} %collective-permute-done.4.refs_0_.refs_4_), channel_id=1, source_target_pairs={{0,7},{1,0},{2,1},{3,2},{4,3},{5,4},{6,5},{7,6},{8,15},{9,8},{10,9... | collective-permute-start | bytes 1572872 | tf_op jit(solution)/shard_map/ppermute | solution.py:386
  49.8 23.9 %collective-permute-start.5 = (bf16[4,2,128,256]{3,2,1,0:T(8,128)(2,1)}, bf16[4,2,128,256]{3,2,1,0:T(8,128)(2,1)S(1)}, u32[]{:S(2)}, u32[]{:S(2)}) collective-permute-start(bf16[4,2,128,256]{3,2,1,0:T(8,128)(2,1)} %copy-done.7), channel_id=1, source_target_pairs={{0,1},{1,2},{2,3},{3,4},{4,5},{5,6},{6,7},{7,0},{8,9},{9,10},{10,1... | collective-permute-start | bytes 1572872 | tf_op jit(solution)/shard_map/ppermute | solution.py:386
  51.4 1.0 copy-start.5
  52.5 1.0 copy-start.8
  73.8 6.4 %collective-permute-start.8 = (bf16[2,2,128,256]{3,2,1,0:T(8,128)(2,1)S(1)}, bf16[2,2,128,256]{3,2,1,0:T(8,128)(2,1)S(1)}, u32[]{:S(2)}, u32[]{:S(2)}) collective-permute-start(bf16[2,2,128,256]{3,2,1,0:T(8,128)(2,1)S(1)} %slice.19), channel_id=1, source_target_pairs={{0,7},{1,0},{2,1},{3,2},{4,3},{5,4},{6,5},{7,6},{8,15},{9,8},{10,9... | collective-permute-start | bytes 786440 | tf_op jit(solution)/shard_map/ppermute | solution.py:386
  73.8 7.7 %collective-permute-start.7 = (bf16[2,2,128,256]{3,2,1,0:T(8,128)(2,1)S(1)}, bf16[2,2,128,256]{3,2,1,0:T(8,128)(2,1)S(1)}, u32[]{:S(2)}, u32[]{:S(2)}) collective-permute-start(bf16[2,2,128,256]{3,2,1,0:T(8,128)(2,1)S(1)} %slice.18), channel_id=1, source_target_pairs={{0,1},{1,2},{2,3},{3,4},{4,5},{5,6},{6,7},{7,0},{8,9},{9,10},{10,1... | collective-permute-start | bytes 786440 | tf_op jit(solution)/shard_map/ppermute | solution.py:386
  81.5 17.6 %copy-start.17 = (s32[2,1,16]{2,1,0:T(1,128)S(1)}, s32[2,1,16]{2,1,0:T(1,128)}, u32[]{:S(2)}) copy-start(s32[2,1,16]{2,1,0:T(1,128)} %param.15) | copy-start | bytes 388
  92.6 1.0 copy-start.3
  93.6 0.7 copy-start.10
  94.3 18.0 %all-to-all-start.2 = ((bf16[4,128,1024]{2,1,0:T(8,128)(2,1)}), bf16[4,128,1024]{2,1,0:T(8,128)(2,1)S(1)}, u32[]{:S(2)}, u32[]{:S(2)}) async-start(bf16[4,128,1024]{2,1,0:T(8,128)(2,1)} %copy-done.3), calls=%async_computation.2 | async-start | bytes 2097152 | tf_op jit(solution)/shard_map/all_to_all | solution.py:406
  99.1 1.0 copy-start.6
  100.2 1.0 copy-start.9
  101.2 0.9 copy-start.11
  104.9 1.3 %collective-permute-start.9 = (bf16[4,16,128]{2,1,0:T(8,128)(2,1)S(1)}, bf16[4,16,128]{2,1,0:T(8,128)(2,1)S(1)}, u32[]{:S(2)}, u32[]{:S(2)}) collective-permute-start(bf16[4,16,128]{2,1,0:T(8,128)(2,1)S(1)} %decode_taken.1), channel_id=1, source_target_pairs={{0,128},{128,0},{1,129},{129,1},{2,130},{130,2},{3,131},{131,3},{4... | collective-permute-start | bytes 49160 | tf_op jit(solution)/shard_map/ppermute | solution.py:451

commit v3 on v2

--- a/solution.py
+++ b/solution.py
@@ -432,7 +432,7 @@
     up1, down1, their_q, their_k, their_v = together((up1, down1, their_q, their_k, their_v))
     up2, down2 = along_z(up1, 1), along_z(down1, -1)
     own = decode_cached(ints, qd.reshape(lists), kn, vn, cache_k[0, 0], cache_v[0, 0], up1)
-    up2, down2, queries, own = together((up2, down2, queries, own))
+    down2, queries, own = together((down2, queries, own))
     up3, down3 = along_z(up2, 1), along_z(down2, -1)
     near, near_at = [own_kv, up1, down1, up2], [0, -1, 1, -2]
     lines, acc = stage(ints, queries, near_at, near)
@@ -441,7 +441,6 @@
     far, far_at = [down2, up3, down3], [2, -3, 3, 4]
     out = stage(ints, queries, far_at, far, ends, (lines, acc))
 
-    their_q, out = together((their_q, out))
     theirs = decode_taken(
         ints, their_q, their_k, their_v, near + far, ends, near_at + far_at
     )

time: 114 us -> 109 us (0.956)
  the two profiles are of different devices: /device:TPU:16 before, /device:TPU:8 now
where the time goes in v3:
time: 109 us
  starting transfers between devices  37.6 us (34%)
  Pallas kernels  32 us (29%)
  waiting for transfers between devices  20.7 us (19%)
  local copies, waits for them, and re-layouts  14.3 us (13%)
  other arithmetic  2.92 us (3%)
    pallas_call x2, Pallas kernels, stage(): pl.pallas_call(functools.partial(stage_kernel, offsets, start, last), gri...  22.1 us
    all_to_all x3, starting transfers between devices, along_x(): lax.all_to_all(value, 'ctx', 0, 0, axis_index_groups=ALONG_X, tiled=True)  21 us
    ppermute x8, starting transfers between devices, along_z(): return lax.ppermute(value, 'ctx', pairs)  16.4 us
    unnamed x31, local copies, waits for them, and re-layouts  12.7 us
    all_to_all x3, waiting for transfers between devices, along_x(): lax.all_to_all(value, 'ctx', 0, 0, axis_index_groups=ALONG_X, tiled=True)  10.9 us
    ppermute x8, waiting for transfers between devices, along_z(): return lax.ppermute(value, 'ctx', pairs)  7.58 us
    pallas_call x1, Pallas kernels, decode_cached(): pl.pallas_call(cached_kernel, grid_spec=grid, out_shape=jax.ShapeDtypeStr...  4.3 us
    pallas_call x3, Pallas kernels, move(): pl.pallas_call(functools.partial(move_kernel, plan), in_specs=[space] * l...  2.83 us
  transfers between devices with their start and end apart: 13, of which 6 were waited for; matrix products, arithmetic and copies ran while one was open for 5% of the time, Pallas kernels for 18%

profile of v3, /device:TPU:8, one launch (start us, length us, event | category | flops | bytes accessed | tf_op | source)
XLA Modules:
  0.0 108.5 jit_solution(4086539318318925873)
XLA Ops:
  0.6 0.9 copy-done.9
  1.6 0.9 copy-done.10
  2.5 0.8 pack_kv.1
  3.4 4.3 %all-to-all-start = ((bf16[4,2,128,256]{3,2,1,0:T(8,128)(2,1)}), bf16[4,2,128,256]{3,2,1,0:T(8,128)(2,1)S(1)}, u32[]{:S(2)}, u32[]{:S(2)}) async-start(bf16[4,2,128,256]{3,2,1,0:T(8,128)(2,1)} %pack_kv.1), calls=%async_computation | async-start | bytes 1048576 | tf_op jit(solution)/shard_map/all_to_all | solution.py:406
  8.2 1.3 %reduce.6 = s32[2,2]{1,0:T(2,128)S(1)} reduce(s32[2,1,2]{2,1,0:T(1,128)} %param.14, s32[]{:T(128)} %broadcast.12), dimensions={1}, to_apply=%param.14.reduce_sub_computation.3 | reduce | bytes 36 | tf_op args[3]
  9.6 1.3 %reduce.7 = s32[2,16]{1,0:T(2,128)S(1)} reduce(s32[2,1,16]{2,1,0:T(1,128)} %param.15, s32[]{:T(128)} %broadcast.12), dimensions={1}, to_apply=%param.15.reduce_sub_computation.3 | reduce | bytes 260 | tf_op args[4]
  11.8 5.4 %all-to-all-done.refs_0_ = bf16[4,2,128,256]{3,2,1,0:T(8,128)(2,1)S(1)} async-done(((bf16[4,2,128,256]{3,2,1,0:T(8,128)(2,1)}), bf16[4,2,128,256]{3,2,1,0:T(8,128)(2,1)S(1)}, u32[]{:S(2)}, u32[]{:S(2)}) %all-to-all-start) | async-done | bytes 524320 | tf_op jit(solution)/shard_map/all_to_all | solution.py:406
  17.2 1.9 %collective-permute-start = (bf16[4,2,128,256]{3,2,1,0:T(8,128)(2,1)S(1)}, bf16[4,2,128,256]{3,2,1,0:T(8,128)(2,1)S(1)}, u32[]{:S(2)}, u32[]{:S(2)}) collective-permute-start(bf16[4,2,128,256]{3,2,1,0:T(8,128)(2,1)S(1)} %all-to-all-done.refs_0_), channel_id=1, source_target_pairs={{0,1},{1,2},{2,3},{3,4},{4,5},{5,6},{6,7},{7,0},{8,9},{9,10},{10,1... | collective-permute-start | bytes 1572872 | tf_op jit(solution)/shard_map/ppermute | solution.py:386
  19.1 3.9 %collective-permute-start.1 = (bf16[4,2,128,256]{3,2,1,0:T(8,128)(2,1)S(1)}, bf16[4,2,128,256]{3,2,1,0:T(8,128)(2,1)S(1)}, u32[]{:S(2)}, u32[]{:S(2)}) collective-permute-start(bf16[4,2,128,256]{3,2,1,0:T(8,128)(2,1)S(1)} %all-to-all-done.refs_0_), channel_id=1, source_target_pairs={{0,7},{1,0},{2,1},{3,2},{4,3},{5,4},{6,5},{7,6},{8,15},{9,8},{10,9... | collective-permute-start | bytes 1572872 | tf_op jit(solution)/shard_map/ppermute | solution.py:386
  23.0 1.2 %copy-done.2 = bf16[1,1,128,4096]{3,2,1,0:T(8,128)(2,1)S(1)} copy-done((bf16[1,1,128,4096]{3,2,1,0:T(8,128)(2,1)S(1)}, bf16[1,1,128,4096]{3,2,1,0:T(8,128)(2,1)}, u32[]{:S(2)}) %copy-start.2) | copy-done | bytes 1048600
  24.3 1.0 pack_q.1
  25.3 3.5 %all-to-all-start.1 = ((bf16[4,128,1024]{2,1,0:T(8,128)(2,1)}), bf16[4,128,1024]{2,1,0:T(8,128)(2,1)S(1)}, u32[]{:S(2)}, u32[]{:S(2)}) async-start(bf16[4,128,1024]{2,1,0:T(8,128)(2,1)} %pack_q.1), calls=%async_computation.1 | async-start | bytes 2097152 | tf_op jit(solution)/shard_map/all_to_all | solution.py:406
  29.0 1.2 %collective-permute-done.2 = bf16[4,4,768]{2,1,0:T(4,128)(2,1)S(1)} collective-permute-done((bf16[4,4,768]{2,1,0:T(4,128)(2,1)S(1)}, bf16[4,4,768]{2,1,0:T(4,128)(2,1)S(1)}, u32[]{:S(2)}, u32[]{:S(2)}) %collective-permute-start.2) | collective-permute-done | bytes 24608 | tf_op jit(solution)/shard_map/ppermute | solution.py:428
  30.2 3.3 %collective-permute-done.after_ref.refs_1_ = bf16[4,2,128,256]{3,2,1,0:T(8,128)(2,1)S(1)} collective-permute-done((bf16[4,2,128,256]{3,2,1,0:T(8,128)(2,1)S(1)}, bf16[4,2,128,256]{3,2,1,0:T(8,128)(2,1)S(1)}, u32[]{:S(2)}, u32[]{:S(2)}) %collective-permute-start) | collective-permute-done | bytes 524320 | tf_op jit(solution)/shard_map/ppermute | solution.py:386
  33.5 3.0 %collective-permute-start.3 = (bf16[4,2,128,256]{3,2,1,0:T(8,128)(2,1)S(1)}, bf16[4,2,128,256]{3,2,1,0:T(8,128)(2,1)}, u32[]{:S(2)}, u32[]{:S(2)}) collective-permute-start(bf16[4,2,128,256]{3,2,1,0:T(8,128)(2,1)S(1)} %collective-permute-done.1.refs_2_), channel_id=1, source_target_pairs={{0,7},{1,0},{2,1},{3,2},{4,3},{5,4},{6,5},{7,6},{8,15},{9,8},{10,9... | collective-permute-start | bytes 1572872 | tf_op jit(solution)/shard_map/ppermute | solution.py:386
  36.5 2.2 %copy-done = bf16[1,1,4,4096,128]{4,3,2,1,0:T(8,128)(2,1)S(1)} copy-done((bf16[1,1,4,4096,128]{4,3,2,1,0:T(8,128)(2,1)S(1)}, bf16[1,1,4,4096,128]{4,3,2,1,0:T(8,128)(2,1)}, u32[]{:S(2)}) %copy-start) | copy-done | bytes 4194328
  38.6 2.2 %copy-done.1 = bf16[1,1,4,4096,128]{4,3,2,1,0:T(8,128)(2,1)S(1)} copy-done((bf16[1,1,4,4096,128]{4,3,2,1,0:T(8,128)(2,1)S(1)}, bf16[1,1,4,4096,128]{4,3,2,1,0:T(8,128)(2,1)}, u32[]{:S(2)}) %copy-start.1) | copy-done | bytes 4194328
  40.8 4.3 %decode_cached.1 = bf16[4,16,128]{2,1,0:T(8,128)(2,1)S(1)} custom-call(s32[54]{0:T(128)S(1)} %concatenate.6.ints, bf16[4,16,128]{2,1,0:T(8,128)(2,1)S(1)} %reshape_squeeze.3.q_ref, bf16[4,4,128]{2,1,0:T(4,128)(2,1)S(1)} %bitcast.22, bf16[4,4,128]{2,1,0:T(4,128)(2,1)S(1)} %bitcast.20, bf16[4,4096,128]{2,1,0:T(8,128)(2,1)S(1)} %bitcast.14, ...), custom_call_target="tpu_custom_call" | custom-call | flops 134217728 | bytes 8388608 | tf_op jit(solution)/shard_map/decode_cached/pallas_call | solution.py:310
  45.2 3.8 %collective-permute-start.6 = (bf16[4,2,128,256]{3,2,1,0:T(8,128)(2,1)}, bf16[4,2,128,256]{3,2,1,0:T(8,128)(2,1)S(1)}, u32[]{:S(2)}, u32[]{:S(2)}) collective-permute-start(bf16[4,2,128,256]{3,2,1,0:T(8,128)(2,1)} %collective-permute-done.3.refs_0_.refs_4_), channel_id=1, source_target_pairs={{0,7},{1,0},{2,1},{3,2},{4,3},{5,4},{6,5},{7,6},{8,15},{9,8},{10,9... | collective-permute-start | bytes 1572872 | tf_op jit(solution)/shard_map/ppermute | solution.py:386
  49.0 1.0 copy-done.5
  50.1 11.0 %prefill_begin.1 = (f32[8,8,512]{2,1,0:T(8,128)S(1)}, f32[8,512,128]{2,1,0:T(8,128)S(1)}) custom-call(s32[54]{0:T(128)S(1)} %concatenate.6.ints, bf16[4,128,1024]{2,1,0:T(8,128)(2,1)S(1)} %all-to-all-done.1.q_ref, bf16[4,2,128,256]{3,2,1,0:T(8,128)(2,1)S(1)} %all-to-all-done.refs_0_, bf16[4,2,128,256]{3,2,1,0:T(8,128)(2,1)S(1)} %collective-permute-done.after_ref.refs_1_, ...), custom_call_target="tpu_custom_call" | custom-call | flops 1879048192 | bytes 8388608 | tf_op jit(solution)/shard_map/prefill_begin/pallas_call | solution.py:243
  61.2 3.7 %collective-permute-start.8 = (bf16[2,2,128,256]{3,2,1,0:T(8,128)(2,1)S(1)}, bf16[2,2,128,256]{3,2,1,0:T(8,128)(2,1)S(1)}, u32[]{:S(2)}, u32[]{:S(2)}) collective-permute-start(bf16[2,2,128,256]{3,2,1,0:T(8,128)(2,1)S(1)} %slice.19), channel_id=1, source_target_pairs={{0,7},{1,0},{2,1},{3,2},{4,3},{5,4},{6,5},{7,6},{8,15},{9,8},{10,9... | collective-permute-start | bytes 786440 | tf_op jit(solution)/shard_map/ppermute | solution.py:386
  64.9 4.2 %collective-permute-done.7.refs_3_.refs_7_ = bf16[2,2,128,256]{3,2,1,0:T(8,128)(2,1)S(1)} collective-permute-done((bf16[2,2,128,256]{3,2,1,0:T(8,128)(2,1)S(1)}, bf16[2,2,128,256]{3,2,1,0:T(8,128)(2,1)S(1)}, u32[]{:S(2)}, u32[]{:S(2)}) %collective-permute-start.7) | collective-permute-done | bytes 262176 | tf_op jit(solution)/shard_map/ppermute | solution.py:386
  69.1 11.1 %prefill_end.1 = bf16[4,128,1024]{2,1,0:T(8,128)(2,1)S(1)} custom-call(s32[54]{0:T(128)S(1)} %concatenate.6.ints, bf16[4,128,1024]{2,1,0:T(8,128)(2,1)S(1)} %all-to-all-done.1.q_ref, bf16[4,2,128,256]{3,2,1,0:T(8,128)(2,1)} %collective-permute-done.3.refs_0_.refs_4_, bf16[4,2,128,256]{3,2,1,0:T(8,128)(2,1)S(1)} %collective-permute-done.5.refs_1_.refs_5_, ...), custom_call_target="tpu_custom_call" | custom-call | flops 1879048192 | bytes 8388608 | tf_op jit(solution)/shard_map/prefill_end/pallas_call | solution.py:243
  80.2 1.0 copy-done.3
  81.9 13.2 %all-to-all-start.2 = ((bf16[4,128,1024]{2,1,0:T(8,128)(2,1)}), bf16[4,128,1024]{2,1,0:T(8,128)(2,1)S(1)}, u32[]{:S(2)}, u32[]{:S(2)}) async-start(bf16[4,128,1024]{2,1,0:T(8,128)(2,1)} %copy-done.3), calls=%async_computation.2 | async-start | bytes 2097152 | tf_op jit(solution)/shard_map/all_to_all | solution.py:406
  95.1 1.0 copy-done.6
  96.2 0.9 copy-done.8
  97.1 2.8 %decode_taken.1 = bf16[4,16,128]{2,1,0:T(8,128)(2,1)S(1)} custom-call(s32[54]{0:T(128)S(1)} %concatenate.6.ints, bf16[4,16,128]{2,1,0:T(8,128)(2,1)S(1)} %reshape.25.q_ref, bf16[4,4,128]{2,1,0:T(4,128)(2,1)S(1)} %get-tuple-element.31.kn_ref, bf16[4,4,128]{2,1,0:T(4,128)(2,1)S(1)} %get-tuple-element.32.vn_ref, ...), custom_call_target="tpu_custom_call" | custom-call | flops 134217728 | bytes 2097152 | tf_op jit(solution)/shard_map/decode_taken/pallas_call | solution.py:372
  100.2 1.0 collective-permute-done.9
  101.9 5.5 %all-to-all-done.2.refs_0_ = bf16[4,128,1024]{2,1,0:T(8,128)(2,1)S(1)} async-done(((bf16[4,128,1024]{2,1,0:T(8,128)(2,1)}), bf16[4,128,1024]{2,1,0:T(8,128)(2,1)S(1)}, u32[]{:S(2)}, u32[]{:S(2)}) %all-to-all-start.2) | async-done | bytes 1048608 | tf_op jit(solution)/shard_map/all_to_all | solution.py:406
  107.4 1.0 assemble.1
  (49 shorter events, 3.5 us)
Async XLA Ops:
  0.6 1.0 copy-start.9
  1.6 0.9 copy-start.10
  2.5 26.3 %copy-start.11 = (bf16[1,1,4,4,128]{4,3,2,1,0:T(4,128)(2,1)S(1)}, bf16[1,1,4,4,128]{4,3,2,1,0:T(4,128)(2,1)}, u32[]{:S(2)}) copy-start(bf16[1,1,4,4,128]{4,3,2,1,0:T(4,128)(2,1)} %param.21) | copy-start | bytes 12292
  2.5 26.3 %copy-start.12 = (bf16[1,1,4,4,128]{4,3,2,1,0:T(4,128)(2,1)S(1)}, bf16[1,1,4,4,128]{4,3,2,1,0:T(4,128)(2,1)}, u32[]{:S(2)}) copy-start(bf16[1,1,4,4,128]{4,3,2,1,0:T(4,128)(2,1)} %param.20) | copy-start | bytes 12292
  2.5 26.3 %copy-start.13 = (bf16[1,1,4,4,512]{4,3,2,1,0:T(4,128)(2,1)S(1)}, bf16[1,1,4,4,512]{4,3,2,1,0:T(4,128)(2,1)}, u32[]{:S(2)}) copy-start(bf16[1,1,4,4,512]{4,3,2,1,0:T(4,128)(2,1)} %param.19) | copy-start | bytes 49156
  3.4 13.8 %all-to-all-start = ((bf16[4,2,128,256]{3,2,1,0:T(8,128)(2,1)}), bf16[4,2,128,256]{3,2,1,0:T(8,128)(2,1)S(1)}, u32[]{:S(2)}, u32[]{:S(2)}) async-start(bf16[4,2,128,256]{3,2,1,0:T(8,128)(2,1)} %pack_kv.1), calls=%async_computation | async-start | bytes 1048576 | tf_op jit(solution)/shard_map/all_to_all | solution.py:406
  17.2 16.3 %collective-permute-start = (bf16[4,2,128,256]{3,2,1,0:T(8,128)(2,1)S(1)}, bf16[4,2,128,256]{3,2,1,0:T(8,128)(2,1)S(1)}, u32[]{:S(2)}, u32[]{:S(2)}) collective-permute-start(bf16[4,2,128,256]{3,2,1,0:T(8,128)(2,1)S(1)} %all-to-all-done.refs_0_), channel_id=1, source_target_pairs={{0,1},{1,2},{2,3},{3,4},{4,5},{5,6},{6,7},{7,0},{8,9},{9,10},{10,1... | collective-permute-start | bytes 1572872 | tf_op jit(solution)/shard_map/ppermute | solution.py:386
  19.1 14.4 %collective-permute-start.1 = (bf16[4,2,128,256]{3,2,1,0:T(8,128)(2,1)S(1)}, bf16[4,2,128,256]{3,2,1,0:T(8,128)(2,1)S(1)}, u32[]{:S(2)}, u32[]{:S(2)}) collective-permute-start(bf16[4,2,128,256]{3,2,1,0:T(8,128)(2,1)S(1)} %all-to-all-done.refs_0_), channel_id=1, source_target_pairs={{0,7},{1,0},{2,1},{3,2},{4,3},{5,4},{6,5},{7,6},{8,15},{9,8},{10,9... | collective-permute-start | bytes 1572872 | tf_op jit(solution)/shard_map/ppermute | solution.py:386
  23.0 1.2 %copy-start.2 = (bf16[1,1,128,4096]{3,2,1,0:T(8,128)(2,1)S(1)}, bf16[1,1,128,4096]{3,2,1,0:T(8,128)(2,1)}, u32[]{:S(2)}) copy-start(bf16[1,1,128,4096]{3,2,1,0:T(8,128)(2,1)} %param.11) | copy-start | bytes 3145732
  25.3 19.9 %all-to-all-start.1 = ((bf16[4,128,1024]{2,1,0:T(8,128)(2,1)}), bf16[4,128,1024]{2,1,0:T(8,128)(2,1)S(1)}, u32[]{:S(2)}, u32[]{:S(2)}) async-start(bf16[4,128,1024]{2,1,0:T(8,128)(2,1)} %pack_q.1), calls=%async_computation.1 | async-start | bytes 2097152 | tf_op jit(solution)/shard_map/all_to_all | solution.py:406
  28.9 1.3 %collective-permute-start.2 = (bf16[4,4,768]{2,1,0:T(4,128)(2,1)S(1)}, bf16[4,4,768]{2,1,0:T(4,128)(2,1)S(1)}, u32[]{:S(2)}, u32[]{:S(2)}) collective-permute-start(bf16[4,4,768]{2,1,0:T(4,128)(2,1)S(1)} %pad_maximum_fusion), channel_id=1, source_target_pairs={{0,128},{128,0},{1,129},{129,1},{2,130},{130,2},{3,131},{131,3},{4... | collective-permute-start | bytes 73736 | tf_op jit(solution)/shard_map/ppermute | solution.py:428
  33.5 11.7 %copy-start.4 = (bf16[4,2,128,256]{3,2,1,0:T(8,128)(2,1)}, bf16[4,2,128,256]{3,2,1,0:T(8,128)(2,1)S(1)}, u32[]{:S(2)}) copy-start(bf16[4,2,128,256]{3,2,1,0:T(8,128)(2,1)S(1)} %collective-permute-done.1.refs_2_) | copy-start | bytes 1572868
  33.5 11.7 %collective-permute-start.3 = (bf16[4,2,128,256]{3,2,1,0:T(8,128)(2,1)S(1)}, bf16[4,2,128,256]{3,2,1,0:T(8,128)(2,1)}, u32[]{:S(2)}, u32[]{:S(2)}) collective-permute-start(bf16[4,2,128,256]{3,2,1,0:T(8,128)(2,1)S(1)} %collective-permute-done.1.refs_2_), channel_id=1, source_target_pairs={{0,7},{1,0},{2,1},{3,2},{4,3},{5,4},{6,5},{7,6},{8,15},{9,8},{10,9... | collective-permute-start | bytes 1572872 | tf_op jit(solution)/shard_map/ppermute | solution.py:386
  36.4 12.6 %collective-permute-start.4 = (bf16[4,2,128,256]{3,2,1,0:T(8,128)(2,1)S(1)}, bf16[4,2,128,256]{3,2,1,0:T(8,128)(2,1)}, u32[]{:S(2)}, u32[]{:S(2)}) collective-permute-start(bf16[4,2,128,256]{3,2,1,0:T(8,128)(2,1)S(1)} %collective-permute-done.after_ref.refs_1_), channel_id=1, source_target_pairs={{0,1},{1,2},{2,3},{3,4},{4,5},{5,6},{6,7},{7,0},{8,9},{9,10},{10,1... | collective-permute-start | bytes 1572872 | tf_op jit(solution)/shard_map/ppermute | solution.py:386
  36.4 2.2 %copy-start = (bf16[1,1,4,4096,128]{4,3,2,1,0:T(8,128)(2,1)S(1)}, bf16[1,1,4,4096,128]{4,3,2,1,0:T(8,128)(2,1)}, u32[]{:S(2)}) copy-start(bf16[1,1,4,4096,128]{4,3,2,1,0:T(8,128)(2,1)} %param.16) | copy-start | bytes 12582916
  38.6 2.2 %copy-start.1 = (bf16[1,1,4,4096,128]{4,3,2,1,0:T(8,128)(2,1)S(1)}, bf16[1,1,4,4096,128]{4,3,2,1,0:T(8,128)(2,1)}, u32[]{:S(2)}) copy-start(bf16[1,1,4,4096,128]{4,3,2,1,0:T(8,128)(2,1)} %param.17) | copy-start | bytes 12582916
  45.2 15.8 %collective-permute-start.6 = (bf16[4,2,128,256]{3,2,1,0:T(8,128)(2,1)}, bf16[4,2,128,256]{3,2,1,0:T(8,128)(2,1)S(1)}, u32[]{:S(2)}, u32[]{:S(2)}) collective-permute-start(bf16[4,2,128,256]{3,2,1,0:T(8,128)(2,1)} %collective-permute-done.3.refs_0_.refs_4_), channel_id=1, source_target_pairs={{0,7},{1,0},{2,1},{3,2},{4,3},{5,4},{6,5},{7,6},{8,15},{9,8},{10,9... | collective-permute-start | bytes 1572872 | tf_op jit(solution)/shard_map/ppermute | solution.py:386
  49.0 12.1 %collective-permute-start.5 = (bf16[4,2,128,256]{3,2,1,0:T(8,128)(2,1)}, bf16[4,2,128,256]{3,2,1,0:T(8,128)(2,1)S(1)}, u32[]{:S(2)}, u32[]{:S(2)}) collective-permute-start(bf16[4,2,128,256]{3,2,1,0:T(8,128)(2,1)} %collective-permute-done.4.refs_3_), channel_id=1, source_target_pairs={{0,1},{1,2},{2,3},{3,4},{4,5},{5,6},{6,7},{7,0},{8,9},{9,10},{10,1... | collective-permute-start | bytes 1572872 | tf_op jit(solution)/shard_map/ppermute | solution.py:386
  49.0 1.0 copy-start.5
  61.1 8.0 %collective-permute-start.7 = (bf16[2,2,128,256]{3,2,1,0:T(8,128)(2,1)S(1)}, bf16[2,2,128,256]{3,2,1,0:T(8,128)(2,1)S(1)}, u32[]{:S(2)}, u32[]{:S(2)}) collective-permute-start(bf16[2,2,128,256]{3,2,1,0:T(8,128)(2,1)S(1)} %slice.18), channel_id=1, source_target_pairs={{0,1},{1,2},{2,3},{3,4},{4,5},{5,6},{6,7},{7,0},{8,9},{9,10},{10,1... | collective-permute-start | bytes 786440 | tf_op jit(solution)/shard_map/ppermute | solution.py:386
  61.2 7.9 %collective-permute-start.8 = (bf16[2,2,128,256]{3,2,1,0:T(8,128)(2,1)S(1)}, bf16[2,2,128,256]{3,2,1,0:T(8,128)(2,1)S(1)}, u32[]{:S(2)}, u32[]{:S(2)}) collective-permute-start(bf16[2,2,128,256]{3,2,1,0:T(8,128)(2,1)S(1)} %slice.19), channel_id=1, source_target_pairs={{0,7},{1,0},{2,1},{3,2},{4,3},{5,4},{6,5},{7,6},{8,15},{9,8},{10,9... | collective-permute-start | bytes 786440 | tf_op jit(solution)/shard_map/ppermute | solution.py:386
  69.1 26.0 %copy-start.14 = (s32[2,1,16]{2,1,0:T(1,128)S(1)}, s32[2,1,16]{2,1,0:T(1,128)}, u32[]{:S(2)}) copy-start(s32[2,1,16]{2,1,0:T(1,128)} %param.15) | copy-start | bytes 388
  80.2 1.0 copy-start.3
  81.2 0.7 copy-start.7
  81.9 25.5 %all-to-all-start.2 = ((bf16[4,128,1024]{2,1,0:T(8,128)(2,1)}), bf16[4,128,1024]{2,1,0:T(8,128)(2,1)S(1)}, u32[]{:S(2)}, u32[]{:S(2)}) async-start(bf16[4,128,1024]{2,1,0:T(8,128)(2,1)} %copy-done.3), calls=%async_computation.2 | async-start | bytes 2097152 | tf_op jit(solution)/shard_map/all_to_all | solution.py:406
  95.1 1.0 copy-start.6
  96.2 0.9 copy-start.8
  99.9 1.3 %collective-permute-start.9 = (bf16[4,16,128]{2,1,0:T(8,128)(2,1)S(1)}, bf16[4,16,128]{2,1,0:T(8,128)(2,1)S(1)}, u32[]{:S(2)}, u32[]{:S(2)}) collective-permute-start(bf16[4,16,128]{2,1,0:T(8,128)(2,1)S(1)} %decode_taken.1), channel_id=1, source_target_pairs={{0,128},{128,0},{1,129},{129,1},{2,130},{130,2},{3,131},{131,3},{4... | collective-permute-start | bytes 49160 | tf_op jit(solution)/shard_map/ppermute | solution.py:450
